TPU v7x, 512 devices: a whole 4x8x8 slice. The times are simulated.
512 devices in a mesh: seq: 128 (over y, z, core), head: 4 (over x).
Axes of the slice: x: 4, y: 8, z: 8, core: 2. Of those that a mesh axis runs over, the one named last changes fastest.
Arguments:
- queries: bfloat16 [16384, 2048], P('seq', 'head'), may hold values from -18 to 18
- keys: bfloat16 [16384, 2048], P('seq', 'head'), may hold values from -12 to 12
- values: bfloat16 [16384, 2048], P('seq', 'head'), may hold values from -12 to 12
- norm_gain: float32 [2048], P('head'), may hold values from 0.1 to 1.9
- out_weight: bfloat16 [2048, 2048], P('head'), may hold values from -0.1875 to 0.1875
Outputs:
- mixed: bfloat16 [16384, 2048], P('seq', 'head')
All inputs are finite; a program needn't handle non-finite values.
Results may differ from a plain program's by a relative error of at most 0.015.
Values may be sent and summed in bfloat16 or wider, within the bound.
No kernel may reach another device: no remote copies, remote signals or barrier semaphores. Data moves between devices by JAX's collectives and lax.ppermute only.
A program may use at most 64 MiB of HBM per device.

v0:
```python
import math

import jax
import jax.numpy as jnp
from jax import lax
from jax.sharding import PartitionSpec as P

HEAD_DIM = 128
BLOCK = 64


inv_root = 1.0 / math.sqrt(2.0)
reach_limit = 7
eps_value = 1e-06


def passed_along(shard, axis, by):
    devices = lax.axis_size(axis)
    pairs = [(i, i + by) for i in range(devices) if 0 <= i + by < devices]
    return lax.ppermute(shard, axis, pairs)


def padded(block, sides, width):
    for axis, dim in sides:
        count = lax.axis_size(axis)
        forward = [(i, i + 1) for i in range(count - 1)]
        backward = [(target, source) for source, target in forward]
        low = lax.ppermute(
            lax.slice_in_dim(block, block.shape[dim] - width, None, axis=dim), axis, forward
        )
        high = lax.ppermute(lax.slice_in_dim(block, 0, width, axis=dim), axis, backward)
        block = jnp.concatenate([low, block, high], axis=dim)
    return block


def restrict(blocked):
    pairs = blocked.reshape(blocked.shape[:-2] + (blocked.shape[-2] // 2, 2, blocked.shape[-1]))
    summed = pairs[..., 0, :].astype(jnp.float32) + pairs[..., 1, :].astype(jnp.float32)
    return (summed * inv_root).astype(jnp.bfloat16)


def partial_softmax(query_rows, key_rows, value_rows, allowed, head_count):
    query_heads = query_rows.reshape(query_rows.shape[:-1] + (head_count, -1))
    key_heads = key_rows.reshape(key_rows.shape[:-1] + (head_count, -1))
    value_heads = value_rows.reshape(value_rows.shape[:-1] + (head_count, -1))
    scaling = 1.0 / math.sqrt(query_heads.shape[-1])
    scores = (
        jnp.einsum(
            "...rhd,...whd->...hrw", query_heads, key_heads, preferred_element_type=jnp.float32
        )
        * scaling
    )
    masked = jnp.where(allowed[..., None, :, :], scores, -jnp.inf)
    highest = jnp.max(masked, axis=-1)
    weights = jnp.exp(masked - highest[..., None])
    totals = jnp.sum(weights, axis=-1)
    summed = jnp.einsum(
        "...hrw,...whd->...rhd",
        weights.astype(jnp.bfloat16),
        value_heads,
        preferred_element_type=jnp.float32,
    )
    return (jnp.swapaxes(highest, -1, -2), jnp.swapaxes(totals, -1, -2), summed)


def merge_pieces(current, incoming):
    largest = jnp.maximum(current[0], incoming[0])
    older = jnp.exp(current[0] - largest)
    newer = jnp.exp(incoming[0] - largest)
    return (
        largest,
        current[1] * older + incoming[1] * newer,
        current[2] * older[..., None] + incoming[2] * newer[..., None],
    )


def far_mask(query_first, query_count, columns, level_rows):
    query_block = (query_first + jnp.arange(query_count, dtype=jnp.int32)) // BLOCK
    key_block = columns // BLOCK
    offset = key_block[None, :] - query_block[:, None]
    is_even = (query_block % 2 == 0)[:, None]
    pattern = (
        (offset == -2)
        | (offset == 2)
        | is_even & (offset == 3)
        | jnp.logical_not(is_even) & (offset == -3)
    )
    inside = (columns >= 0) & (columns < level_rows)
    return pattern & inside[None, :]


def neighbour_window(paired, reach_count, level_local, position):
    fetched = {}
    for distance in list(range(1, reach_count + 1)) + list(range(-reach_count, 0)):
        fetched[distance] = passed_along(paired, "seq", distance)
    below_pieces = [fetched[distance] for distance in range(reach_count, 0, -1)]
    above_pieces = [fetched[-distance] for distance in range(1, reach_count + 1)]
    window = jnp.concatenate(below_pieces + [paired] + above_pieces, axis=1)
    columns = (position - reach_count) * level_local + jnp.arange(window.shape[1], dtype=jnp.int32)
    return (window, columns)


def shards(queries, keys, values, norm_gain, out_weight):
    tokens_here, features = queries.shape
    head_count = features // HEAD_DIM
    seq_devices = lax.axis_size("seq")
    position = lax.axis_index("seq")
    seq_length = tokens_here * seq_devices
    level_count = (seq_length // (4 * BLOCK)).bit_length() - 1
    leaf_blocks = tokens_here // BLOCK
    stacked = jnp.stack([keys, values])
    rimmed = padded(stacked, (("seq", 1),), BLOCK)
    windows = jnp.concatenate(
        [
            rimmed[:, slot_index * BLOCK : slot_index * BLOCK + tokens_here].reshape(
                2, leaf_blocks, BLOCK, features
            )
            for slot_index in range(3)
        ],
        axis=2,
    )
    global_block = (
        position * leaf_blocks
        + jnp.arange(leaf_blocks, dtype=jnp.int32)[:, None]
        + jnp.arange(3 * BLOCK, dtype=jnp.int32)[None, :] // BLOCK
        - 1
    )
    leaf_valid = (global_block >= 0) & (global_block < seq_length // BLOCK)
    near = partial_softmax(
        queries.reshape(leaf_blocks, BLOCK, features),
        windows[0],
        windows[1],
        leaf_valid[:, None, :],
        head_count,
    )
    state = (
        near[0].reshape(tokens_here, head_count),
        near[1].reshape(tokens_here, head_count),
        near[2].reshape(tokens_here, head_count, HEAD_DIM),
    )
    reaches = []
    for level_id in range(1, level_count + 1):
        level_local = tokens_here >> level_id
        extent = max(3 * BLOCK, 4 * BLOCK - level_local)
        reaches.append(-(-extent // level_local))
    far_first = level_count + 1
    for level_id in range(level_count, 0, -1):
        if reaches[level_id - 1] > reach_limit:
            far_first = level_id
    query_levels = [queries]
    pair_levels = [stacked]
    for level_id in range(1, level_count + 1):
        query_levels.append(restrict(query_levels[-1]))
        pair_levels.append(restrict(pair_levels[-1]))
    prepared = {}
    far_range = range(far_first, level_count + 1)
    for level_id in far_range:
        whole = lax.all_gather(pair_levels[level_id], "seq", axis=1, tiled=True)
        prepared[level_id] = (whole, jnp.arange(whole.shape[1], dtype=jnp.int32))
    for level_id in range(1, level_count + 1):
        level_local = tokens_here >> level_id
        level_rows = seq_length >> level_id
        if level_id in prepared:
            window, columns = prepared[level_id]
        else:
            window, columns = neighbour_window(
                pair_levels[level_id], reaches[level_id - 1], level_local, position
            )
        allowed = far_mask(position * level_local, level_local, columns, level_rows)
        level_piece = partial_softmax(
            query_levels[level_id], window[0], window[1], allowed, head_count
        )
        factor = 2**level_id
        level_piece = tuple((jnp.repeat(member, factor, axis=0) for member in level_piece))
        state = merge_pieces(state, level_piece)
    attended = (state[2] / state[1][..., None]).reshape(tokens_here, features).astype(jnp.bfloat16)
    widened = attended.astype(jnp.float32)
    squares = lax.psum(jnp.sum(widened * widened, axis=1), "head")
    mean_square = squares / (features * lax.axis_size("head"))
    normed = (widened * lax.rsqrt(mean_square + eps_value)[:, None] * norm_gain).astype(
        jnp.bfloat16
    )
    mixed_rows = lax.psum_scatter(
        lax.dot_general(
            out_weight, normed, (((0,), (1,)), ((), ())), preferred_element_type=jnp.float32
        ),
        "head",
        scatter_dimension=0,
        tiled=True,
    )
    return mixed_rows.T.astype(jnp.bfloat16)


def solution(mesh):
    return jax.shard_map(
        shards,
        mesh=mesh,
        in_specs=(P("seq", "head"), P("seq", "head"), P("seq", "head"), P("head"), P("head", None)),
        out_specs=P("seq", "head"),
        check_vma=False,
    )
```

profile of v0, /device:TPU:8, one launch (start us, length us, event | category | flops | bytes accessed | tf_op | source)
XLA Modules:
  0.0 428.1 jit_solution(18257304012381574687)
XLA Ops:
  11.2 10.2 %collective-permute-start.21 = (bf16[2,32,512]{2,1,0:T(8,128)(2,1)}, bf16[2,32,512]{2,1,0:T(8,128)(2,1)}, u32[]{:S(2)}, u32[]{:S(2)}) collective-permute-start(bf16[2,32,512]{2,1,0:T(8,128)(2,1)} %bitcast.333), channel_id=1, source_target_pairs={{28,0},{32,4},{36,8},{40,12},{44,16},{48,20},{52,24},{56,28},{60,3... | collective-permute-start | bytes 196616 | tf_op jit(solution)/shard_map/ppermute | solution.py:20
  21.4 2.5 collective-permute-start.20
  23.9 1.9 collective-permute-start.19
  25.8 4.5 %collective-permute-start.18 = (bf16[2,32,512]{2,1,0:T(8,128)(2,1)}, bf16[2,32,512]{2,1,0:T(8,128)(2,1)}, u32[]{:S(2)}, u32[]{:S(2)}) collective-permute-start(bf16[2,32,512]{2,1,0:T(8,128)(2,1)} %bitcast.333), channel_id=1, source_target_pairs={{16,0},{20,4},{24,8},{28,12},{32,16},{36,20},{40,24},{44,28},{48,3... | collective-permute-start | bytes 196616 | tf_op jit(solution)/shard_map/ppermute | solution.py:20
  30.3 3.2 collective-permute-start.8
  49.9 55.6 %all-gather.3 = bf16[2,256,1,512]{3,0,2,1:T(2,128)(2,1)S(1)} all-gather(bf16[2,2,1,512]{3,0,2,1:T(2,128)(2,1)S(1)} %multiply_convert_fusion.9), channel_id=5, replica_groups=mesh['seq'=128,'head'=4] {'seq'}, dimensions={1}, use_global_device_ids=true | all-gather | bytes 528384 | tf_op jit(solution)/shard_map/all_gather | solution.py:158
  126.1 2.7 collective-permute-start.9
  129.7 8.4 %collective-permute-done.9 = bf16[2,32,512]{2,1,0:T(8,128)(2,1)S(1)} collective-permute-done((bf16[2,32,512]{2,1,0:T(8,128)(2,1)}, bf16[2,32,512]{2,1,0:T(8,128)(2,1)S(1)}, u32[]{:S(2)}, u32[]{:S(2)}) %collective-permute-start.9) | collective-permute-done | bytes 65568 | tf_op jit(solution)/shard_map/ppermute | solution.py:20
  138.2 1.9 collective-permute-start.10
  140.1 8.1 %collective-permute-done.10 = bf16[2,32,512]{2,1,0:T(8,128)(2,1)S(1)} collective-permute-done((bf16[2,32,512]{2,1,0:T(8,128)(2,1)}, bf16[2,32,512]{2,1,0:T(8,128)(2,1)S(1)}, u32[]{:S(2)}, u32[]{:S(2)}) %collective-permute-start.10) | collective-permute-done | bytes 65568 | tf_op jit(solution)/shard_map/ppermute | solution.py:20
  148.3 1.9 collective-permute-start.11
  150.2 8.0 %collective-permute-done.11 = bf16[2,32,512]{2,1,0:T(8,128)(2,1)S(1)} collective-permute-done((bf16[2,32,512]{2,1,0:T(8,128)(2,1)}, bf16[2,32,512]{2,1,0:T(8,128)(2,1)S(1)}, u32[]{:S(2)}, u32[]{:S(2)}) %collective-permute-start.11) | collective-permute-done | bytes 65568 | tf_op jit(solution)/shard_map/ppermute | solution.py:20
  158.2 1.9 collective-permute-start.12
  160.2 7.2 %collective-permute-done.12 = bf16[2,32,512]{2,1,0:T(8,128)(2,1)S(1)} collective-permute-done((bf16[2,32,512]{2,1,0:T(8,128)(2,1)}, bf16[2,32,512]{2,1,0:T(8,128)(2,1)S(1)}, u32[]{:S(2)}, u32[]{:S(2)}) %collective-permute-start.12) | collective-permute-done | bytes 65568 | tf_op jit(solution)/shard_map/ppermute | solution.py:20
  167.4 3.0 collective-permute-start.13
  170.4 5.8 %collective-permute-done.13 = bf16[2,32,512]{2,1,0:T(8,128)(2,1)S(1)} collective-permute-done((bf16[2,32,512]{2,1,0:T(8,128)(2,1)}, bf16[2,32,512]{2,1,0:T(8,128)(2,1)S(1)}, u32[]{:S(2)}, u32[]{:S(2)}) %collective-permute-start.13) | collective-permute-done | bytes 65568 | tf_op jit(solution)/shard_map/ppermute | solution.py:20
  176.2 1.9 collective-permute-start.14
  178.2 6.0 %collective-permute-done.14 = bf16[2,32,512]{2,1,0:T(8,128)(2,1)S(1)} collective-permute-done((bf16[2,32,512]{2,1,0:T(8,128)(2,1)}, bf16[2,32,512]{2,1,0:T(8,128)(2,1)S(1)}, u32[]{:S(2)}, u32[]{:S(2)}) %collective-permute-start.14) | collective-permute-done | bytes 65568 | tf_op jit(solution)/shard_map/ppermute | solution.py:20
  184.1 1.9 collective-permute-start.15
  186.1 2.2 collective-permute-done.15
  190.2 4.4 %collective-permute-done.16 = bf16[2,32,512]{2,1,0:T(8,128)(2,1)S(1)} collective-permute-done((bf16[2,32,512]{2,1,0:T(8,128)(2,1)}, bf16[2,32,512]{2,1,0:T(8,128)(2,1)S(1)}, u32[]{:S(2)}, u32[]{:S(2)}) %collective-permute-start.16) | collective-permute-done | bytes 65568 | tf_op jit(solution)/shard_map/ppermute | solution.py:20
  194.6 4.3 collective-permute-start.17
  198.9 2.2 collective-permute-done.17
  201.1 6.6 %collective-permute-start.7 = (bf16[2,64,512]{2,1,0:T(8,128)(2,1)}, bf16[2,64,512]{2,1,0:T(8,128)(2,1)}, u32[]{:S(2)}, u32[]{:S(2)}) collective-permute-start(bf16[2,64,512]{2,1,0:T(8,128)(2,1)} %fusion.194), channel_id=1, source_target_pairs={{12,0},{16,4},{20,8},{24,12},{28,16},{32,20},{36,24},{40,28},{44,3... | collective-permute-start | bytes 393224 | tf_op jit(solution)/shard_map/ppermute | solution.py:20
  207.7 1.9 collective-permute-start.6
  210.5 4.5 %collective-permute-start.5 = (bf16[2,64,512]{2,1,0:T(8,128)(2,1)}, bf16[2,64,512]{2,1,0:T(8,128)(2,1)}, u32[]{:S(2)}, u32[]{:S(2)}) collective-permute-start(bf16[2,64,512]{2,1,0:T(8,128)(2,1)} %fusion.194), channel_id=1, source_target_pairs={{4,0},{8,4},{12,8},{16,12},{20,16},{24,20},{28,24},{32,28},{36,32}... | collective-permute-start | bytes 393224 | tf_op jit(solution)/shard_map/ppermute | solution.py:20
  215.8 2.0 collective-permute-start
  218.7 5.6 %collective-permute-start.1 = (bf16[2,64,512]{2,1,0:T(8,128)(2,1)S(1)}, bf16[2,64,512]{2,1,0:T(8,128)(2,1)}, u32[]{:S(2)}, u32[]{:S(2)}) collective-permute-start(bf16[2,64,512]{2,1,0:T(8,128)(2,1)S(1)} %get-tuple-element.52), channel_id=1, source_target_pairs={{4,0},{8,4},{12,8},{16,12},{20,16},{24,20},{28,24},{32,28},{36,32}... | collective-permute-start | bytes 393224 | tf_op jit(solution)/shard_map/ppermute | solution.py:31
  231.7 2.0 reshape_squeeze.47
  235.7 1.9 collective-permute-start.3
  237.6 1.9 collective-permute-start.2
  240.7 8.2 %collective-permute-done.2 = bf16[2,64,512]{2,1,0:T(8,128)(2,1)S(1)} collective-permute-done((bf16[2,64,512]{2,1,0:T(8,128)(2,1)}, bf16[2,64,512]{2,1,0:T(8,128)(2,1)S(1)}, u32[]{:S(2)}, u32[]{:S(2)}) %collective-permute-start.2) | collective-permute-done | bytes 131104 | tf_op jit(solution)/shard_map/ppermute | solution.py:20
  248.9 3.0 collective-permute-start.4
  254.2 3.5 collective-permute-done.4
  276.0 4.2 fusion.171
  280.2 3.5 copy.398
  286.9 2.3 copy.399
  291.0 6.9 %fusion.170 = (bf16[1,1024,1,512]{3,0,2,1:T(2,128)(2,1)}, bf16[1,1024,1,512]{3,0,2,1:T(2,128)(2,1)}) fusion(bf16[2,1024,1,512]{3,0,2,1:T(2,128)(2,1)} %all-gather.10.cloned.1.call-done), kind=kLoop, calls=%fused_computation.391 | loop fusion | bytes 4194304 | tf_op jit(solution)/shard_map/slice | solution.py:171
  298.0 4.6 %copy.396 = bf16[1,1024,1,512]{1,3,2,0:T(8,128)(2,1)S(1)} copy(bf16[1,1024,1,512]{3,0,2,1:T(2,128)(2,1)} %get-tuple-element.38) | data formatting | bytes 2097152
  304.8 4.6 %copy.397 = bf16[1,1024,1,512]{1,3,2,0:T(8,128)(2,1)S(1)} copy(bf16[1,1024,1,512]{3,0,2,1:T(2,128)(2,1)} %get-tuple-element.37) | data formatting | bytes 2097152
  310.4 9.9 %fusion.169 = (bf16[1,2048,1,512]{3,0,2,1:T(2,128)(2,1)}, bf16[1,2048,1,512]{3,0,2,1:T(2,128)(2,1)}) fusion(bf16[2,2048,1,512]{3,0,2,1:T(2,128)(2,1)} %all-gather.8.cloned.1.call-done), kind=kLoop, calls=%fused_computation.390 | loop fusion | bytes 8388608 | tf_op jit(solution)/shard_map/slice | solution.py:171
  320.3 10.6 %copy.392 = bf16[1,2048,1,512]{1,3,2,0:T(8,128)(2,1)} copy(bf16[1,2048,1,512]{3,0,2,1:T(2,128)(2,1)} %get-tuple-element.36) | data formatting | bytes 4194304
  330.8 2.1 fusion.181
  334.3 10.6 %copy.393 = bf16[1,2048,1,512]{1,3,2,0:T(8,128)(2,1)} copy(bf16[1,2048,1,512]{3,0,2,1:T(2,128)(2,1)} %get-tuple-element.35) | data formatting | bytes 4194304
  345.0 2.4 convolution_bitcast_fusion.4
  366.2 2.6 multiply_reduce_fusion
  368.9 10.8 %psum.7 = f32[128]{0:T(128)S(1)} all-reduce(f32[128]{0:T(128)S(1)} %reduce_sum.82), channel_id=1, replica_groups=mesh['seq'=128,'head'=4] {'head'}, use_global_device_ids=true, to_apply=%region_15.16 | all-reduce | flops 128 | bytes 1024 | tf_op jit(solution)/shard_map/psum | solution.py:178
  385.7 34.3 %reduce-scatter.2.cloned.1.call-done = f32[512,128]{0,1:T(8,128)} async-done(((f32[2048,128]{0,1:T(8,128)}), f32[512,128]{0,1:T(8,128)}) %reduce-scatter.2.cloned.1.call-update) | async-done | bytes 262160 | tf_op jit(solution)/shard_map/reduce_scatter | solution.py:183
  (353 shorter events, 113.5 us)
Async XLA Ops:
  6.5 377.3 %copy-start = (bf16[512,2048]{1,0:T(8,128)(2,1)S(1)}, bf16[512,2048]{1,0:T(8,128)(2,1)}, u32[]{:S(2)}) copy-start(bf16[512,2048]{1,0:T(8,128)(2,1)} %param.9) | copy-start | bytes 6291460
  6.5 41.2 %copy-start.12 = (bf16[128,512]{1,0:T(8,128)(2,1)S(1)}, bf16[128,512]{1,0:T(8,128)(2,1)}, u32[]{:S(2)}) copy-start(bf16[128,512]{1,0:T(8,128)(2,1)} %param.5) | copy-start | bytes 393220
  6.5 269.5 %all-gather.12.cloned.1.call-start = ((), (), s32[]{:S(2)}) async-start(), calls=%async_computation.4 | async-start | bytes 1056768 | tf_op jit(solution)/shard_map/all_gather | solution.py:158
  9.0 38.1 %copy-start.5 = (bf16[2,32,1,512]{3,0,2,1:T(2,128)(2,1)}, bf16[2,32,1,512]{3,0,2,1:T(2,128)(2,1)S(1)}, u32[]{:S(2)}) copy-start(bf16[2,32,1,512]{3,0,2,1:T(2,128)(2,1)S(1)} %multiply_convert_fusion.3) | copy-start | bytes 196612
  9.0 24.4 %copy-start.16 = (bf16[2,16,1,512]{3,0,2,1:T(2,128)(2,1)}, bf16[2,16,1,512]{3,0,2,1:T(2,128)(2,1)S(1)}, u32[]{:S(2)}) copy-start(bf16[2,16,1,512]{3,0,2,1:T(2,128)(2,1)S(1)} %multiply_convert_fusion.5) | copy-start | bytes 98308
  9.7 281.3 %all-gather.10.cloned.1.call-start = ((), (), s32[]{:S(2)}) async-start(), calls=%async_computation.3 | async-start | bytes 2113536 | tf_op jit(solution)/shard_map/all_gather | solution.py:158
  10.5 299.9 %all-gather.8.cloned.1.call-start = ((), (), s32[]{:S(2)}) async-start(), calls=%async_computation.2 | async-start | bytes 4227072 | tf_op jit(solution)/shard_map/all_gather | solution.py:158
  11.2 207.6 %collective-permute-start.21 = (bf16[2,32,512]{2,1,0:T(8,128)(2,1)}, bf16[2,32,512]{2,1,0:T(8,128)(2,1)}, u32[]{:S(2)}, u32[]{:S(2)}) collective-permute-start(bf16[2,32,512]{2,1,0:T(8,128)(2,1)} %bitcast.333), channel_id=1, source_target_pairs={{28,0},{32,4},{36,8},{40,12},{44,16},{48,20},{52,24},{56,28},{60,3... | collective-permute-start | bytes 196616 | tf_op jit(solution)/shard_map/ppermute | solution.py:20
  21.4 194.4 %collective-permute-start.20 = (bf16[2,32,512]{2,1,0:T(8,128)(2,1)}, bf16[2,32,512]{2,1,0:T(8,128)(2,1)}, u32[]{:S(2)}, u32[]{:S(2)}) collective-permute-start(bf16[2,32,512]{2,1,0:T(8,128)(2,1)} %bitcast.333), channel_id=1, source_target_pairs={{24,0},{28,4},{32,8},{36,12},{40,16},{44,20},{48,24},{52,28},{56,3... | collective-permute-start | bytes 196616 | tf_op jit(solution)/shard_map/ppermute | solution.py:20
  23.9 186.6 %collective-permute-start.19 = (bf16[2,32,512]{2,1,0:T(8,128)(2,1)}, bf16[2,32,512]{2,1,0:T(8,128)(2,1)}, u32[]{:S(2)}, u32[]{:S(2)}) collective-permute-start(bf16[2,32,512]{2,1,0:T(8,128)(2,1)} %bitcast.333), channel_id=1, source_target_pairs={{20,0},{24,4},{28,8},{32,12},{36,16},{40,20},{44,24},{48,28},{52,3... | collective-permute-start | bytes 196616 | tf_op jit(solution)/shard_map/ppermute | solution.py:20
  25.8 181.9 %collective-permute-start.18 = (bf16[2,32,512]{2,1,0:T(8,128)(2,1)}, bf16[2,32,512]{2,1,0:T(8,128)(2,1)}, u32[]{:S(2)}, u32[]{:S(2)}) collective-permute-start(bf16[2,32,512]{2,1,0:T(8,128)(2,1)} %bitcast.333), channel_id=1, source_target_pairs={{16,0},{20,4},{24,8},{28,12},{32,16},{36,20},{40,24},{44,28},{48,3... | collective-permute-start | bytes 196616 | tf_op jit(solution)/shard_map/ppermute | solution.py:20
  30.3 95.8 %collective-permute-start.8 = (bf16[2,32,512]{2,1,0:T(8,128)(2,1)}, bf16[2,32,512]{2,1,0:T(8,128)(2,1)}, u32[]{:S(2)}, u32[]{:S(2)}) collective-permute-start(bf16[2,32,512]{2,1,0:T(8,128)(2,1)} %bitcast.333), channel_id=1, source_target_pairs={{0,28},{4,32},{8,36},{12,40},{16,44},{20,48},{24,52},{28,56},{32,6... | collective-permute-start | bytes 196616 | tf_op jit(solution)/shard_map/ppermute | solution.py:20
  33.5 386.5 %reduce-scatter.2.cloned.1.call-start = ((), (), s32[]{:S(2)}) async-start(), calls=%async_computation.1 | async-start | bytes 1310720 | tf_op jit(solution)/shard_map/reduce_scatter | solution.py:183
  106.3 19.9 %copy-start.1 = (bf16[128,512]{1,0:T(8,128)(2,1)S(1)}, bf16[128,512]{1,0:T(8,128)(2,1)}, u32[]{:S(2)}) copy-start(bf16[128,512]{1,0:T(8,128)(2,1)} %param.6) | copy-start | bytes 393220
  107.4 18.7 %copy-start.2 = (bf16[128,512]{1,0:T(8,128)(2,1)S(1)}, bf16[128,512]{1,0:T(8,128)(2,1)}, u32[]{:S(2)}) copy-start(bf16[128,512]{1,0:T(8,128)(2,1)} %param.7) | copy-start | bytes 393220
  107.4 78.7 %copy-start.6 = (bf16[2,32,1,512]{3,0,2,1:T(2,128)(2,1)S(1)}, bf16[2,32,1,512]{3,0,2,1:T(2,128)(2,1)}, u32[]{:S(2)}) copy-start(bf16[2,32,1,512]{3,0,2,1:T(2,128)(2,1)} %copy-done.5) | copy-start | bytes 196612
  126.1 12.0 %collective-permute-start.9 = (bf16[2,32,512]{2,1,0:T(8,128)(2,1)}, bf16[2,32,512]{2,1,0:T(8,128)(2,1)S(1)}, u32[]{:S(2)}, u32[]{:S(2)}) collective-permute-start(bf16[2,32,512]{2,1,0:T(8,128)(2,1)} %bitcast.333), channel_id=1, source_target_pairs={{0,24},{4,28},{8,32},{12,36},{16,40},{20,44},{24,48},{28,52},{32,5... | collective-permute-start | bytes 196616 | tf_op jit(solution)/shard_map/ppermute | solution.py:20
  138.2 10.1 %collective-permute-start.10 = (bf16[2,32,512]{2,1,0:T(8,128)(2,1)}, bf16[2,32,512]{2,1,0:T(8,128)(2,1)S(1)}, u32[]{:S(2)}, u32[]{:S(2)}) collective-permute-start(bf16[2,32,512]{2,1,0:T(8,128)(2,1)} %bitcast.333), channel_id=1, source_target_pairs={{0,20},{4,24},{8,28},{12,32},{16,36},{20,40},{24,44},{28,48},{32,5... | collective-permute-start | bytes 196616 | tf_op jit(solution)/shard_map/ppermute | solution.py:20
  148.3 9.9 %collective-permute-start.11 = (bf16[2,32,512]{2,1,0:T(8,128)(2,1)}, bf16[2,32,512]{2,1,0:T(8,128)(2,1)S(1)}, u32[]{:S(2)}, u32[]{:S(2)}) collective-permute-start(bf16[2,32,512]{2,1,0:T(8,128)(2,1)} %bitcast.333), channel_id=1, source_target_pairs={{0,16},{4,20},{8,24},{12,28},{16,32},{20,36},{24,40},{28,44},{32,4... | collective-permute-start | bytes 196616 | tf_op jit(solution)/shard_map/ppermute | solution.py:20
  158.2 9.2 %collective-permute-start.12 = (bf16[2,32,512]{2,1,0:T(8,128)(2,1)}, bf16[2,32,512]{2,1,0:T(8,128)(2,1)S(1)}, u32[]{:S(2)}, u32[]{:S(2)}) collective-permute-start(bf16[2,32,512]{2,1,0:T(8,128)(2,1)} %bitcast.333), channel_id=1, source_target_pairs={{0,12},{4,16},{8,20},{12,24},{16,28},{20,32},{24,36},{28,40},{32,4... | collective-permute-start | bytes 196616 | tf_op jit(solution)/shard_map/ppermute | solution.py:20
  167.4 8.8 %collective-permute-start.13 = (bf16[2,32,512]{2,1,0:T(8,128)(2,1)}, bf16[2,32,512]{2,1,0:T(8,128)(2,1)S(1)}, u32[]{:S(2)}, u32[]{:S(2)}) collective-permute-start(bf16[2,32,512]{2,1,0:T(8,128)(2,1)} %bitcast.333), channel_id=1, source_target_pairs={{0,8},{4,12},{8,16},{12,20},{16,24},{20,28},{24,32},{28,36},{32,40... | collective-permute-start | bytes 196616 | tf_op jit(solution)/shard_map/ppermute | solution.py:20
  176.2 7.9 %collective-permute-start.14 = (bf16[2,32,512]{2,1,0:T(8,128)(2,1)}, bf16[2,32,512]{2,1,0:T(8,128)(2,1)S(1)}, u32[]{:S(2)}, u32[]{:S(2)}) collective-permute-start(bf16[2,32,512]{2,1,0:T(8,128)(2,1)} %bitcast.333), channel_id=1, source_target_pairs={{0,4},{4,8},{8,12},{12,16},{16,20},{20,24},{24,28},{28,32},{32,36}... | collective-permute-start | bytes 196616 | tf_op jit(solution)/shard_map/ppermute | solution.py:20
  178.2 48.9 %copy-start.15 = (bf16[32,512]{1,0:T(8,128)(2,1)S(1)}, bf16[32,512]{1,0:T(8,128)(2,1)}, u32[]{:S(2)}) copy-start(bf16[32,512]{1,0:T(8,128)(2,1)} %copy-done.14) | copy-start | bytes 98308
  184.1 4.1 collective-permute-start.15
  188.3 6.4 %collective-permute-start.16 = (bf16[2,32,512]{2,1,0:T(8,128)(2,1)}, bf16[2,32,512]{2,1,0:T(8,128)(2,1)S(1)}, u32[]{:S(2)}, u32[]{:S(2)}) collective-permute-start(bf16[2,32,512]{2,1,0:T(8,128)(2,1)} %bitcast.333), channel_id=1, source_target_pairs={{8,0},{12,4},{16,8},{20,12},{24,16},{28,20},{32,24},{36,28},{40,32... | collective-permute-start | bytes 196616 | tf_op jit(solution)/shard_map/ppermute | solution.py:20
  194.6 6.5 %collective-permute-start.17 = (bf16[2,32,512]{2,1,0:T(8,128)(2,1)}, bf16[2,32,512]{2,1,0:T(8,128)(2,1)S(1)}, u32[]{:S(2)}, u32[]{:S(2)}) collective-permute-start(bf16[2,32,512]{2,1,0:T(8,128)(2,1)} %bitcast.333), channel_id=1, source_target_pairs={{12,0},{16,4},{20,8},{24,12},{28,16},{32,20},{36,24},{40,28},{44,3... | collective-permute-start | bytes 196616 | tf_op jit(solution)/shard_map/ppermute | solution.py:20
  201.1 66.7 %collective-permute-start.7 = (bf16[2,64,512]{2,1,0:T(8,128)(2,1)}, bf16[2,64,512]{2,1,0:T(8,128)(2,1)}, u32[]{:S(2)}, u32[]{:S(2)}) collective-permute-start(bf16[2,64,512]{2,1,0:T(8,128)(2,1)} %fusion.194), channel_id=1, source_target_pairs={{12,0},{16,4},{20,8},{24,12},{28,16},{32,20},{36,24},{40,28},{44,3... | collective-permute-start | bytes 393224 | tf_op jit(solution)/shard_map/ppermute | solution.py:20
  207.7 58.5 %collective-permute-start.6 = (bf16[2,64,512]{2,1,0:T(8,128)(2,1)}, bf16[2,64,512]{2,1,0:T(8,128)(2,1)}, u32[]{:S(2)}, u32[]{:S(2)}) collective-permute-start(bf16[2,64,512]{2,1,0:T(8,128)(2,1)} %fusion.194), channel_id=1, source_target_pairs={{8,0},{12,4},{16,8},{20,12},{24,16},{28,20},{32,24},{36,28},{40,32... | collective-permute-start | bytes 393224 | tf_op jit(solution)/shard_map/ppermute | solution.py:20
  210.5 51.9 %collective-permute-start.5 = (bf16[2,64,512]{2,1,0:T(8,128)(2,1)}, bf16[2,64,512]{2,1,0:T(8,128)(2,1)}, u32[]{:S(2)}, u32[]{:S(2)}) collective-permute-start(bf16[2,64,512]{2,1,0:T(8,128)(2,1)} %fusion.194), channel_id=1, source_target_pairs={{4,0},{8,4},{12,8},{16,12},{20,16},{24,20},{28,24},{32,28},{36,32}... | collective-permute-start | bytes 393224 | tf_op jit(solution)/shard_map/ppermute | solution.py:20
  215.8 19.8 %collective-permute-start = (bf16[2,64,512]{2,1,0:T(8,128)(2,1)S(1)}, bf16[2,64,512]{2,1,0:T(8,128)(2,1)S(1)}, u32[]{:S(2)}, u32[]{:S(2)}) collective-permute-start(bf16[2,64,512]{2,1,0:T(8,128)(2,1)S(1)} %get-tuple-element.51), channel_id=1, source_target_pairs={{0,4},{4,8},{8,12},{12,16},{16,20},{20,24},{24,28},{28,32},{32,36}... | collective-permute-start | bytes 393224 | tf_op jit(solution)/shard_map/ppermute | solution.py:28
  218.7 18.9 %collective-permute-start.1 = (bf16[2,64,512]{2,1,0:T(8,128)(2,1)S(1)}, bf16[2,64,512]{2,1,0:T(8,128)(2,1)}, u32[]{:S(2)}, u32[]{:S(2)}) collective-permute-start(bf16[2,64,512]{2,1,0:T(8,128)(2,1)S(1)} %get-tuple-element.52), channel_id=1, source_target_pairs={{4,0},{8,4},{12,8},{16,12},{20,16},{24,20},{28,24},{32,28},{36,32}... | collective-permute-start | bytes 393224 | tf_op jit(solution)/shard_map/ppermute | solution.py:31
  235.7 16.9 %collective-permute-start.3 = (bf16[2,64,512]{2,1,0:T(8,128)(2,1)}, bf16[2,64,512]{2,1,0:T(8,128)(2,1)}, u32[]{:S(2)}, u32[]{:S(2)}) collective-permute-start(bf16[2,64,512]{2,1,0:T(8,128)(2,1)} %fusion.194), channel_id=1, source_target_pairs={{0,8},{4,12},{8,16},{12,20},{16,24},{20,28},{24,32},{28,36},{32,40... | collective-permute-start | bytes 393224 | tf_op jit(solution)/shard_map/ppermute | solution.py:20
  237.6 11.2 %collective-permute-start.2 = (bf16[2,64,512]{2,1,0:T(8,128)(2,1)}, bf16[2,64,512]{2,1,0:T(8,128)(2,1)S(1)}, u32[]{:S(2)}, u32[]{:S(2)}) collective-permute-start(bf16[2,64,512]{2,1,0:T(8,128)(2,1)} %fusion.194), channel_id=1, source_target_pairs={{0,12},{4,16},{8,20},{12,24},{16,28},{20,32},{24,36},{28,40},{32,4... | collective-permute-start | bytes 393224 | tf_op jit(solution)/shard_map/ppermute | solution.py:20
  248.9 8.8 %collective-permute-start.4 = (bf16[2,64,512]{2,1,0:T(8,128)(2,1)}, bf16[2,64,512]{2,1,0:T(8,128)(2,1)}, u32[]{:S(2)}, u32[]{:S(2)}) collective-permute-start(bf16[2,64,512]{2,1,0:T(8,128)(2,1)} %fusion.194), channel_id=1, source_target_pairs={{0,4},{4,8},{8,12},{12,16},{16,20},{20,24},{24,28},{28,32},{32,36}... | collective-permute-start | bytes 393224 | tf_op jit(solution)/shard_map/ppermute | solution.py:20
  344.9 20.1 %copy-start.40 = (f32[2,4,64]{2,1,0:T(4,128)S(1)}, f32[2,4,64]{2,1,0:T(4,128)}, u32[]{:S(2)}) copy-start(f32[2,4,64]{2,1,0:T(4,128)} %copy-done.39) | copy-start | bytes 6148
  344.9 20.1 %copy-start.47 = (f32[2,64,4]{1,0,2:T(2,128)S(1)}, f32[2,64,4]{1,0,2:T(2,128)}, u32[]{:S(2)}) copy-start(f32[2,64,4]{1,0,2:T(2,128)} %reshape.1580) | copy-start | bytes 6148
  344.9 20.1 %copy-start.48 = (f32[2,64,4]{1,2,0:T(4,128)S(1)}, f32[2,64,4]{1,2,0:T(4,128)}, u32[]{:S(2)}) copy-start(f32[2,64,4]{1,2,0:T(4,128)} %copy.359) | copy-start | bytes 6148
  344.9 20.1 %copy-start.49 = (f32[2,64,4]{1,0,2:T(2,128)S(1)}, f32[2,64,4]{1,0,2:T(2,128)}, u32[]{:S(2)}) copy-start(f32[2,64,4]{1,0,2:T(2,128)} %reshape.1584) | copy-start | bytes 6148
  344.9 20.1 %copy-start.44 = (f32[2,4,64]{2,1,0:T(4,128)S(1)}, f32[2,4,64]{2,1,0:T(4,128)}, u32[]{:S(2)}) copy-start(f32[2,4,64]{2,1,0:T(4,128)} %copy-done.43) | copy-start | bytes 6148
  344.9 20.9 %copy-start.4 = (f32[64,4,128]{2,0,1:T(8,128)S(1)}, f32[64,4,128]{2,0,1:T(8,128)}, u32[]{:S(2)}) copy-start(f32[64,4,128]{2,0,1:T(8,128)} %copy-done.3) | copy-start | bytes 393220
  344.9 21.0 %copy-start.8 = (f32[32,4,128]{2,0,1:T(8,128)S(1)}, f32[32,4,128]{2,0,1:T(8,128)}, u32[]{:S(2)}) copy-start(f32[32,4,128]{2,0,1:T(8,128)} %copy-done.7) | copy-start | bytes 196612
  344.9 21.1 %copy-start.38 = (f32[4,4,128]{2,0,1:T(4,128)S(1)}, f32[4,4,128]{2,0,1:T(4,128)}, u32[]{:S(2)}) copy-start(f32[4,4,128]{2,0,1:T(4,128)} %copy-done.37) | copy-start | bytes 24580
  345.0 21.1 %copy-start.30 = (f32[8,4,128]{2,0,1:T(8,128)S(1)}, f32[8,4,128]{2,0,1:T(8,128)}, u32[]{:S(2)}) copy-start(f32[8,4,128]{2,0,1:T(8,128)} %copy-done.29) | copy-start | bytes 49156
  345.0 21.2 %copy-start.13 = (bf16[2,192,4,128]{3,2,1,0:T(4,128)(2,1)S(1)}, bf16[2,192,4,128]{3,2,1,0:T(4,128)(2,1)}, u32[]{:S(2)}) copy-start(bf16[2,192,4,128]{3,2,1,0:T(4,128)(2,1)} %reshape_squeeze.42) | copy-start | bytes 1179652
  347.3 18.8 %copy-start.11 = (f32[2,4,64,192]{3,2,1,0:T(8,128)S(1)}, f32[2,4,64,192]{3,2,1,0:T(8,128)}, u32[]{:S(2)}) copy-start(f32[2,4,64,192]{3,2,1,0:T(8,128)} %copy-done.10) | copy-start | bytes 1179652
  366.2 14.9 %copy-start.51 = (f32[4,4,128]{2,1,0:T(4,128)S(1)}, f32[4,4,128]{2,1,0:T(4,128)}, u32[]{:S(2)}) copy-start(f32[4,4,128]{2,1,0:T(4,128)} %copy.406) | copy-start | bytes 24580
  366.2 14.9 %copy-start.41 = (f32[8,4,128]{2,1,0:T(4,128)S(1)}, f32[8,4,128]{2,1,0:T(4,128)}, u32[]{:S(2)}) copy-start(f32[8,4,128]{2,1,0:T(4,128)} %copy.405) | copy-start | bytes 49156
  366.2 15.0 %copy-start.28 = (f32[128,4]{1,0:T(8,128)S(1)}, f32[128,4]{1,0:T(8,128)}, u32[]{:S(2)}) copy-start(f32[128,4]{1,0:T(8,128)} %copy.352) | copy-start | bytes 6148
  (39 other events, 225.2 us)
Sparse Core Ops, SparseCore 0:
  10.4 87.3 all-gather.11
  100.9 80.7 all-gather.9
  184.8 85.2 all-gather.7
  385.8 34.1 reduce-scatter.1
where the time goes:
time: 431 us; the launch traced here: 428 us
  local copies, waits for them, and re-layouts  124 us (29%)
  waiting for transfers between devices  99.1 us (23%)
  starting transfers between devices  71.3 us (17%)
  blocking collectives  66.4 us (15%)
  other arithmetic  32.7 us (8%)
  matrix products  20 us (5%)
  between operations  14.5 us (3%)
    ppermute x20, waiting for transfers between devices, passed_along(): return lax.ppermute(shard, axis, pairs)  64 us
    ppermute x20, starting transfers between devices, passed_along(): return lax.ppermute(shard, axis, pairs)  63.6 us
    all_gather x1, blocking collectives, shards(): whole = lax.all_gather(pair_levels[level_id], 'seq', axis=1, tiled=True)  55.6 us
    unnamed x156, local copies, waits for them, and re-layouts  52.9 us
    reduce_scatter x1, waiting for transfers between devices, shards(): lax.psum_scatter(lax.dot_general(out_weight, normed, (((0,), (1,)), ((),...  34.3 us
    slice x6, local copies, waits for them, and re-layouts, shards(): window[1]  23.9 us
    psum x1, blocking collectives, shards(): squares = lax.psum(jnp.sum(widened * widened, axis=1), 'head')  10.8 us
    reshape x22, local copies, waits for them, and re-layouts, shards(): jnp.repeat(member, factor, axis=0)  9.58 us
  transfers between devices with their start and end apart: 26, of which 12 were waited for; matrix products, arithmetic and copies ran while one was open for 25% of the time, Pallas kernels for 0%

commit v1 on v0

v1 whole, which is shorter than its diff:
```python
import math

import jax
import jax.numpy as jnp
from jax import lax
from jax.experimental import pallas as pl
from jax.experimental.pallas import tpu as pltpu
from jax.sharding import Mesh
from jax.sharding import PartitionSpec as P

HEAD_DIM = 128
BLOCK = 64
QUADS = 32
TOKENS = 512
PAIR = 2 * HEAD_DIM
eps_value = 1e-06
inv_root = 1.0 / math.sqrt(2.0)
scaling = 1.0 / math.sqrt(HEAD_DIM)
NEG = -1e30
PARAMS = pltpu.CompilerParams(vmem_limit_bytes=48 * 1024 * 1024)
FULL = pltpu.CompilerParams(vmem_limit_bytes=60 * 1024 * 1024)
NEEDED = (
    (2, 3, 6, 4),
    (3, 6, 7, 4),
    (0, 4, 5, 6),
    (0, 1, 5, 6),
    (2, 6, 7, 0),
    (2, 3, 7, 0),
    (4, 0, 1, 2),
    (4, 5, 1, 2),
)


def pair_sums(rows, columns):
    out_row = lax.broadcasted_iota(jnp.int32, (rows, columns), 0)
    in_row = lax.broadcasted_iota(jnp.int32, (rows, columns), 1)
    return ((in_row >> 1) == out_row).astype(jnp.float32).astype(jnp.bfloat16)


def restrict(fine, matrix):
    summed = jnp.dot(matrix, fine, preferred_element_type=jnp.float32)
    return (summed * inv_root).astype(jnp.bfloat16)


def piece(query, key, value, allowed):
    scores = lax.dot_general(
        query, key, (((1,), (1,)), ((), ())), preferred_element_type=jnp.float32
    )
    scores = scores * scaling
    if allowed is not None:
        scores = jnp.where(allowed, scores, NEG)
    highest = jnp.max(scores, axis=1, keepdims=True)
    weights = jnp.exp(scores - highest)
    total = jnp.sum(weights, axis=1, keepdims=True)
    summed = jnp.dot(weights.astype(jnp.bfloat16), value, preferred_element_type=jnp.float32)
    shape = summed.shape
    return jnp.broadcast_to(highest, shape), jnp.broadcast_to(total, shape), summed


def attend(query, pairs, allowed):
    return piece(query, pairs[:, :HEAD_DIM], pairs[:, HEAD_DIM:], allowed)


def merge_pieces(current, incoming):
    largest = jnp.maximum(current[0], incoming[0])
    older = jnp.exp(current[0] - largest)
    newer = jnp.exp(incoming[0] - largest)
    return (
        largest,
        current[1] * older + incoming[1] * newer,
        current[2] * older + incoming[2] * newer,
    )


def spread(state, scratch, rows, factor):
    result = []
    for index, member in enumerate(state):
        for step in range(factor):
            scratch[index, pl.ds(step, rows, stride=factor), :] = member[:rows]
        result.append(scratch[index, : rows * factor, :])
    return tuple(result)


def third_mask(rows, valid):
    block = lax.broadcasted_iota(jnp.int32, (rows, 3 * BLOCK), 1) // BLOCK
    flags = [jnp.where(flag, 1, 0) for flag in valid]
    chosen = jnp.where(block == 0, flags[0], jnp.where(block == 1, flags[1], flags[2]))
    return chosen == 1


def begin_copies(copies, sems):
    started = [
        pltpu.make_async_copy(source, target, sems.at[index])
        for index, (source, target) in enumerate(copies)
    ]
    for copy in started:
        copy.start()
    return started


def wait_copies(started):
    for copy in started:
        copy.wait()


def my_place():
    return lax.axis_index("zl") * 2 + lax.axis_index("c")


def other_place(step):
    high, low = lax.axis_index("zl"), lax.axis_index("c")
    if step & 2:
        high = 1 - high
    if step & 1:
        low = 1 - low
    return high * 2 + low


def open_kernel(queries_ref, keys_ref, values_ref, column_ref, *refs):
    head_refs, pairs_ref, sems = refs[:4], refs[4], refs[5]
    copies = [(keys_ref, pairs_ref.at[:, :512]), (values_ref, pairs_ref.at[:, 512:])]
    for step, head_ref in enumerate(head_refs):
        begin = pl.multiple_of(other_place(step) * HEAD_DIM, HEAD_DIM)
        for index, ref in enumerate((queries_ref, keys_ref, values_ref)):
            columns = slice(index * HEAD_DIM, (index + 1) * HEAD_DIM)
            copies.append((ref.at[:, pl.ds(begin, HEAD_DIM)], head_ref.at[:, columns]))
    started = begin_copies(copies, sems)
    wait_copies(started[:2])
    first = restrict(pairs_ref[...], pair_sums(64, 128))
    third = restrict(restrict(first, pair_sums(32, 64)), pair_sums(16, 32))
    for row in range(8):
        column_ref[row] = third
    wait_copies(started[2:])


def column_kernel(row_ref, needed_ref, column_ref, *refs):
    out_ref = refs[-1]
    row = row_ref[0]
    chosen = [needed_ref[row * 4 + slot] for slot in range(4)]
    chosen.append(chosen[3] + 1)
    rest = jnp.concatenate([column_ref[source] for source in chosen], axis=0)
    fourth = restrict(rest, pair_sums(48, 80))
    fifth = restrict(fourth, pair_sums(32, 48))
    out_row = lax.broadcasted_iota(jnp.int32, (16, 32), 0)
    in_row = lax.broadcasted_iota(jnp.int32, (16, 32), 1)
    kept = (out_row < 12) & (in_row == out_row)
    halved = (out_row >= 12) & (((in_row - 12) >> 1) == out_row - 12)
    matrix = jnp.where(kept | halved, 1.0, 0.0).astype(jnp.bfloat16)
    tail = jnp.dot(matrix, fifth, preferred_element_type=jnp.float32)
    place = lax.broadcasted_iota(jnp.int32, tail.shape, 0)
    tail = jnp.where(place < 12, tail, tail * inv_root).astype(jnp.bfloat16)
    members = [column_ref[lax.rem(row + step + 7, 8)] for step in range(3)] + [tail]
    whole = jnp.concatenate(members, axis=0)
    for head in range(4):
        low = head * HEAD_DIM
        for group in range(4):
            out_ref[group * 4 + head, :, :HEAD_DIM] = whole[:, low : low + HEAD_DIM]
            out_ref[group * 4 + head, :, HEAD_DIM:] = whole[:, 512 + low : 512 + low + HEAD_DIM]


def prepare_kernel(own_ref, one_ref, two_ref, three_ref, *refs):
    x_ref, next_ref, prev_ref, query_ref, sems = refs
    copies = []
    for step, ref in enumerate((own_ref, one_ref, two_ref, three_ref)):
        begin = pl.multiple_of(other_place(step) * 128, 128)
        copies.append((ref, x_ref.at[pl.ds(begin, 128), :]))
    wait_copies(begin_copies(copies, sems))
    x = x_ref[...]
    next_ref[:64] = x[TOKENS - 64 :, HEAD_DIM:]
    prev_ref[:64] = x[:64, HEAD_DIM:]
    first = restrict(x, pair_sums(256, 512))
    next_ref[64:192] = first[128:, HEAD_DIM:]
    prev_ref[64:192] = first[:128, HEAD_DIM:]
    query_ref[:256] = first[:, :HEAD_DIM]
    second = restrict(first, pair_sums(128, 256))
    next_ref[192:] = second[:, HEAD_DIM:]
    prev_ref[192:] = second[:, HEAD_DIM:]
    query_ref[256:384] = second[:, :HEAD_DIM]
    third = restrict(second[:, :HEAD_DIM], pair_sums(64, 128))
    query_ref[384:448] = third
    fourth = restrict(third, pair_sums(32, 64))
    query_ref[448:480] = fourth
    fifth = restrict(fourth, pair_sums(16, 32))
    query_ref[480:496] = fifth
    query_ref[496:512] = restrict(fifth, pair_sums(16, 16))


def block_rows(array, blocks):
    return jnp.concatenate([array[block * BLOCK : (block + 1) * BLOCK] for block in blocks], axis=0)


def far_piece(query, pairs_ref, block, block_count, first=0):
    even = block % 2 == 0
    chosen = (
        jnp.where(even, block - 2, block - 3),
        jnp.where(even, block + 2, block - 2),
        jnp.where(even, block + 3, block + 2),
    )
    valid = [(target >= 0) & (target < block_count) for target in chosen]
    last = pairs_ref.shape[0] // BLOCK - 1
    parts = []
    for target in chosen:
        begin = pl.multiple_of(jnp.clip(target - first, 0, last) * BLOCK, BLOCK)
        parts.append(pairs_ref[pl.ds(begin, BLOCK), :])
    return attend(query, jnp.concatenate(parts, axis=0), third_mask(query.shape[0], valid))


def gather_levels(row, needed_ref, row_ref, third_ref, fourth_ref, fifth_ref, sixth_ref):
    wide, narrow = pair_sums(128, 256), pair_sums(64, 128)
    fifth_ref[...] = jnp.zeros_like(fifth_ref)
    for step in range(3):
        low, high = step * 256, step * 128
        rows = [row_ref[source, step * 16 : (step + 1) * 16] for source in range(16)]
        third = jnp.concatenate(rows, axis=0)
        third_ref[low : low + 256] = third
        fourth = restrict(third, wide)
        fourth_ref[high : high + 128] = fourth
        begin = pl.multiple_of(lax.rem(row + step + 7, 8) * 64, 64)
        fifth_ref[pl.ds(begin, 64), :] = restrict(fourth, narrow)
    tail = jnp.concatenate([row_ref[source, 48:64] for source in range(16)], axis=0)
    out_row = lax.broadcasted_iota(jnp.int32, (256, 256), 0)
    in_row = lax.broadcasted_iota(jnp.int32, (256, 256), 1)
    of_fifth = ((out_row & 63) >> 2) * 16 + (out_row >> 6) * 4 + (out_row & 3)
    of_sixth = ((out_row & 31) >> 1) * 16 + 12 + ((out_row >> 5) & 1) * 2 + (out_row & 1)
    source = jnp.where(out_row < 192, of_fifth, of_sixth)
    matrix = jnp.where(in_row == source, 1.0, 0.0).astype(jnp.bfloat16)
    ordered = jnp.dot(matrix, tail, preferred_element_type=jnp.float32).astype(jnp.bfloat16)
    for slot in range(3):
        begin = pl.multiple_of(needed_ref[row * 4 + slot] * 64, 64)
        fifth_ref[pl.ds(begin, 64), :] = ordered[slot * 64 : (slot + 1) * 64]
    for begin in range(0, 256, 128):
        sixth_ref[begin : begin + 128] = restrict(fifth_ref[2 * begin : 2 * begin + 256], wide)
    begin = pl.multiple_of(needed_ref[row * 4 + 3] * 32, 64)
    sixth_ref[pl.ds(begin, 64), :] = ordered[192:]


def inner_kernel(x_ref, inner_ref):
    x = x_ref[...]
    for block in range(1, 7):
        rows = slice(block * BLOCK, (block + 1) * BLOCK)
        keys = slice((block - 1) * BLOCK, (block + 2) * BLOCK)
        near = attend(x[rows, :HEAD_DIM], x[keys, HEAD_DIM:], None)
        for index, member in enumerate(near):
            inner_ref[index, rows] = member


def far_kernel(quad_ref, needed_ref, query_ref, row_hbm, far_ref, row_ref, *refs):
    *levels, scratch, sems = refs
    started = begin_copies(((row_hbm, row_ref),), sems)
    wait_copies(started)
    quad = quad_ref[0]
    row = quad // 4
    third_ref, fourth_ref, fifth_ref, sixth_ref = levels
    gather_levels(row, needed_ref, row_ref, third_ref, fourth_ref, fifth_ref, sixth_ref)
    state = far_piece(query_ref[496:512], sixth_ref, row // 2, 4)
    state = spread(state, scratch, 8, 2)
    state = merge_pieces(far_piece(query_ref[480:496], fifth_ref, row, 8), state)
    state = spread(state, scratch, 16, 2)
    fourth = far_piece(query_ref[448:480], fourth_ref, quad // 2, 16, 2 * row - 2)
    state = spread(merge_pieces(fourth, state), scratch, 32, 2)
    third = far_piece(query_ref[384:448], third_ref, quad, 32, 4 * row - 4)
    for index, member in enumerate(merge_pieces(third, state)):
        for step in range(2):
            far_ref[index, pl.ds(step, 64, stride=2), :] = member


def attend_kernel(
    quad_ref, x_ref, query_ref, far_ref, inner_ref, prev_hbm, next_hbm, out_ref, *refs
):
    prev_ref, next_ref, scratch, sems = refs
    started = begin_copies(((prev_hbm, prev_ref), (next_hbm, next_ref)), sems)
    wait_copies(started)
    quad = quad_ref[0]
    has_prev = quad > 0
    has_next = quad < QUADS - 1
    x = x_ref[...]
    state = tuple(far_ref[index] for index in range(3))
    prev, later = prev_ref[...], next_ref[...]
    rim = jnp.concatenate([prev[192:], later[192:]], axis=0)
    pieces = []
    for block, chosen, valid in (
        (0, (0, 2, 3), (has_prev, has_next, has_next)),
        (1, (0, 1, 3), (has_prev, has_prev, has_next)),
    ):
        rows = slice(256 + block * BLOCK, 256 + (block + 1) * BLOCK)
        pieces.append(attend(query_ref[rows], block_rows(rim, chosen), third_mask(BLOCK, valid)))
    second = tuple(jnp.concatenate(members, axis=0) for members in zip(*pieces))
    state = spread(merge_pieces(second, state), scratch, 128, 2)
    own = restrict(x[:, HEAD_DIM:], pair_sums(256, 512))
    rim = jnp.concatenate([prev[64:192], own, later[64:192]], axis=0)
    pieces = []
    for block, chosen, valid in (
        (0, (0, 4, 5), (has_prev, True, True)),
        (1, (0, 1, 5), (has_prev, has_prev, True)),
        (2, (2, 6, 7), (True, has_next, has_next)),
        (3, (2, 3, 7), (True, True, has_next)),
    ):
        rows = slice(block * BLOCK, (block + 1) * BLOCK)
        pieces.append(attend(query_ref[rows], block_rows(rim, chosen), third_mask(BLOCK, valid)))
    first = tuple(jnp.concatenate(members, axis=0) for members in zip(*pieces))
    state = spread(merge_pieces(first, state), scratch, 256, 2)
    rim = jnp.concatenate([prev[:64], x[:, HEAD_DIM:], later[:64]], axis=0)
    for block in range(8):
        rows = slice(block * BLOCK, (block + 1) * BLOCK)
        if block in (0, 7):
            valid = (has_prev, True, True) if block == 0 else (True, True, has_next)
            keys = rim[block * BLOCK : (block + 3) * BLOCK]
            near = attend(x[rows, :HEAD_DIM], keys, third_mask(BLOCK, valid))
        else:
            near = tuple(inner_ref[index, rows] for index in range(3))
        _, total, summed = merge_pieces(near, tuple(member[rows] for member in state))
        out_ref[rows] = (summed / total).astype(jnp.bfloat16)


def project_kernel(attended_ref, weight_ref, gain_ref, out_ref):
    rows = jnp.concatenate([attended_ref[head] for head in range(4)], axis=1)
    widened = rows.astype(jnp.float32)
    squares = jnp.sum(widened * widened, axis=1, keepdims=True)
    squares = jnp.transpose(jnp.broadcast_to(squares, (128, 128)))[:16]
    coarse = squares.astype(jnp.bfloat16)
    rest = (squares - coarse.astype(jnp.float32)).astype(jnp.bfloat16)
    gained = (widened * gain_ref[...]).astype(jnp.bfloat16)
    for target in range(4):
        columns = slice(target * 512, (target + 1) * 512)
        product = jnp.dot(gained, weight_ref[:, columns], preferred_element_type=jnp.float32)
        out_ref[target, :128] = product.astype(jnp.bfloat16)
        out_ref[target, 128:, :128] = coarse
        out_ref[target, 128:, 128:256] = rest
        out_ref[target, 128:, 256:] = jnp.zeros((16, 256), jnp.bfloat16)


def sum_kernel(parts_ref, out_ref):
    summed = jnp.zeros((128, 512), jnp.float32)
    squares = jnp.zeros((16, 128), jnp.float32)
    for source in range(4):
        summed = summed + parts_ref[source, :128].astype(jnp.float32)
        squares = squares + parts_ref[source, 128:, :128].astype(jnp.float32)
        squares = squares + parts_ref[source, 128:, 128:256].astype(jnp.float32)
    mean_square = jnp.transpose(jnp.broadcast_to(squares[:1], (128, 128)))[:, :1] * (1.0 / 2048)
    out_ref[...] = (summed * lax.rsqrt(mean_square + eps_value)).astype(jnp.bfloat16)


def shift_pairs(by):
    return [
        (quad * 4 + place, (quad + by) * 4 + place)
        for quad in range(QUADS)
        if 0 <= quad + by < QUADS
        for place in range(4)
    ]


def exchange_pairs(step):
    return [(device, device ^ step) for device in range(4 * QUADS)]


ANYWHERE = pl.BlockSpec(memory_space=pl.ANY)
SCALARS = pl.BlockSpec(memory_space=pltpu.SMEM)


def vmem(count):
    return [pl.BlockSpec(memory_space=pltpu.VMEM)] * count


def bf16(*shape):
    return jax.ShapeDtypeStruct(shape, jnp.bfloat16)


def shards(queries, keys, values, norm_gain, out_weight):
    line = ("y", "zh", "zl", "c")
    row = lax.axis_index("y").astype(jnp.int32)
    quad = row * 4 + lax.axis_index("zh").astype(jnp.int32)
    row, quad = row.reshape(1), quad.reshape(1)
    needed = jnp.array([slot for slots in NEEDED for slot in slots], jnp.int32)
    column, *heads = pl.pallas_call(
        open_kernel,
        out_shape=[bf16(8, 16, 1024)] + [bf16(128, 3 * HEAD_DIM)] * 4,
        in_specs=[ANYWHERE] * 3,
        out_specs=vmem(5),
        scratch_shapes=[
            pltpu.VMEM((128, 1024), jnp.bfloat16),
            pltpu.SemaphoreType.DMA((14,)),
        ],
        compiler_params=FULL,
    )(queries, keys, values)
    column = lax.all_to_all(column, "y", 0, 0, tiled=True)
    for step in range(1, 4):
        heads[step] = lax.ppermute(heads[step], line, exchange_pairs(step))
    row_parts = pl.pallas_call(
        column_kernel,
        out_shape=bf16(16, 64, PAIR),
        in_specs=[SCALARS] * 2 + vmem(1) + [ANYWHERE] * 3,
        out_specs=vmem(1)[0],
        compiler_params=PARAMS,
    )(row, needed, column, *heads[1:])
    row_all = lax.all_to_all(row_parts, ("zh", "zl", "c"), 0, 0, tiled=True)
    x, to_next, to_prev, coarse_queries = pl.pallas_call(
        prepare_kernel,
        out_shape=[
            bf16(TOKENS, 3 * HEAD_DIM),
            bf16(320, PAIR),
            bf16(320, PAIR),
            bf16(512, HEAD_DIM),
        ],
        in_specs=[ANYWHERE] * 4,
        out_specs=vmem(4),
        scratch_shapes=[pltpu.SemaphoreType.DMA((4,))],
        compiler_params=PARAMS,
    )(*heads)
    from_prev = lax.ppermute(to_next, line, shift_pairs(1))
    from_next = lax.ppermute(to_prev, line, shift_pairs(-1))
    inner = pl.pallas_call(
        inner_kernel,
        out_shape=jax.ShapeDtypeStruct((3, TOKENS, HEAD_DIM), jnp.float32),
        in_specs=vmem(1),
        out_specs=vmem(1)[0],
        compiler_params=PARAMS,
    )(x)
    far = pl.pallas_call(
        far_kernel,
        out_shape=jax.ShapeDtypeStruct((3, 128, HEAD_DIM), jnp.float32),
        in_specs=[SCALARS] * 2 + vmem(1) + [ANYWHERE],
        out_specs=vmem(1)[0],
        scratch_shapes=[
            pltpu.VMEM((16, 64, PAIR), jnp.bfloat16),
            pltpu.VMEM((768, PAIR), jnp.bfloat16),
            pltpu.VMEM((384, PAIR), jnp.bfloat16),
            pltpu.VMEM((512, PAIR), jnp.bfloat16),
            pltpu.VMEM((256, PAIR), jnp.bfloat16),
            pltpu.VMEM((3, 128, HEAD_DIM), jnp.float32),
            pltpu.SemaphoreType.DMA((1,)),
        ],
        compiler_params=PARAMS,
    )(quad, needed, coarse_queries, row_all)
    attended = pl.pallas_call(
        attend_kernel,
        out_shape=bf16(TOKENS, HEAD_DIM),
        in_specs=[SCALARS] + vmem(4) + [ANYWHERE] * 2,
        out_specs=vmem(1)[0],
        scratch_shapes=[
            pltpu.VMEM((320, PAIR), jnp.bfloat16),
            pltpu.VMEM((320, PAIR), jnp.bfloat16),
            pltpu.VMEM((3, TOKENS, HEAD_DIM), jnp.float32),
            pltpu.SemaphoreType.DMA((2,)),
        ],
        compiler_params=PARAMS,
    )(quad, x, coarse_queries, far, inner, from_prev, from_next)
    own = lax.all_to_all(attended.reshape(4, 128, HEAD_DIM), ("zl", "c"), 0, 0, tiled=True)
    products = pl.pallas_call(
        project_kernel,
        out_shape=bf16(4, 144, 512),
        in_specs=vmem(3),
        out_specs=vmem(1)[0],
        compiler_params=PARAMS,
    )(own, out_weight, norm_gain.reshape(1, 512))
    parts = lax.all_to_all(products, "x", 0, 0, tiled=True)
    return pl.pallas_call(
        sum_kernel,
        out_shape=bf16(128, 512),
        in_specs=vmem(1),
        out_specs=vmem(1)[0],
        compiler_params=PARAMS,
    )(parts)


def solution(mesh):
    grid = Mesh(mesh.devices.reshape(8, 4, 2, 2, 4), ("y", "zh", "zl", "c", "x"))
    split = P(("y", "zh", "zl", "c"), "x")
    return jax.shard_map(
        shards,
        mesh=grid,
        in_specs=(split, split, split, P("x"), P("x", None)),
        out_specs=split,
        check_vma=False,
    )
```

time: 431 us -> 88.3 us (0.20)
  local copies, waits for them, and re-layouts: 124 us -> 3.39 us
  waiting for transfers between devices: 99.1 us -> 11.1 us
  blocking collectives: 66.4 us -> 23.5 us
  starting transfers between devices: 71.3 us -> 35.2 us
  other arithmetic: 32.7 us -> 0 us
  matrix products: 20 us -> 0 us
  between operations: 14.5 us -> 0.19 us
  Pallas kernels: 0 us -> 14.2 us
    ppermute x22 -> x5, waiting for transfers between devices: 64.1 us -> 3.9 us  [the longest x3 3.89 us: shards(): heads[step] = lax.ppermute(heads[step], line, exchange_pairs(step))]
    all_gather x1 -> x0, blocking collectives: 55.6 us -> none  [shards(): whole = lax.all_gather(pair_levels[level_id], 'seq', axis=1, tiled=True)]
    ppermute x22 -> x5, starting transfers between devices: 71.2 us -> 16.4 us  [the longest x3 7.57 us: shards(): heads[step] = lax.ppermute(heads[step], line, exchange_pairs(step))]
    unnamed x156 -> x16, local copies, waits for them, and re-layouts: 52.9 us -> 3.39 us
    reduce_scatter x1 -> x0, waiting for transfers between devices: 34.3 us -> none  [shards(): lax.psum_scatter(lax.dot_general(out_weight, normed, (((0,), (1,)), ((),...]
    slice x9 -> x0, local copies, waits for them, and re-layouts: 24.1 us -> none  [the longest x6 23.9 us: shards(): window[1]]
    all_to_all x0 -> x2, blocking collectives: none -> 23.5 us  [the longest x1 13.9 us: shards(): parts = lax.all_to_all(products, 'x', 0, 0, tiled=True)]
    dot_general x15 -> x0, matrix products: 20 us -> none  [the longest x7 9.46 us: partial_softmax(): jnp.einsum('...hrw,...whd->...rhd', weights.astype(jnp.bfloat16), value_h...]
  transfers between devices with their start and end apart: 26 -> 7, of which waited for: 12 -> 3; matrix products, arithmetic and copies ran while one was open for 25% -> 0% of each run, Pallas kernels for 0% -> 7%
where the time goes in v1:
time: 88.3 us; the launch traced here: 87.6 us
  starting transfers between devices  35.2 us (40%)
  blocking collectives  23.5 us (27%)
  Pallas kernels  14.2 us (16%)
  waiting for transfers between devices  11.1 us (13%)
  local copies, waits for them, and re-layouts  3.39 us (4%)
    all_to_all x1, blocking collectives, shards(): parts = lax.all_to_all(products, 'x', 0, 0, tiled=True)  13.9 us
    all_to_all x1, blocking collectives, shards(): lax.all_to_all(attended.reshape(4, 128, HEAD_DIM), ('zl', 'c'), 0, 0, til...  9.62 us
    all_to_all x1, starting transfers between devices, shards(): row_all = lax.all_to_all(row_parts, ('zh', 'zl', 'c'), 0, 0, tiled=True)  9.51 us
    all_to_all x1, starting transfers between devices, shards(): column = lax.all_to_all(column, 'y', 0, 0, tiled=True)  9.28 us
    ppermute x3, starting transfers between devices, shards(): heads[step] = lax.ppermute(heads[step], line, exchange_pairs(step))  7.57 us
    all_to_all x1, waiting for transfers between devices, shards(): row_all = lax.all_to_all(row_parts, ('zh', 'zl', 'c'), 0, 0, tiled=True)  7.19 us
    ppermute x1, starting transfers between devices, shards(): from_prev = lax.ppermute(to_next, line, shift_pairs(1))  4.72 us
    ppermute x1, starting transfers between devices, shards(): from_next = lax.ppermute(to_prev, line, shift_pairs(-1))  4.12 us
  transfers between devices with their start and end apart: 7, of which 3 were waited for; matrix products, arithmetic and copies ran while one was open for 0% of the time, Pallas kernels for 7%

profile of v1, /device:TPU:8, one launch (start us, length us, event | category | flops | bytes accessed | tf_op | source)
XLA Modules:
  0.0 87.6 jit_solution(1732206386690814190)
XLA Ops:
  0.0 2.4 %shard_map.64 = (bf16[8,16,1024]{2,1,0:T(8,128)(2,1)}, bf16[128,384]{1,0:T(8,128)(2,1)}, bf16[128,384]{1,0:T(8,128)(2,1)}, bf16[128,384]{1,0:T(8,128)(2,1)}, bf16[128,384]{1,0:T(8,128)(2,1)}) custom-call(bf16[128,512]{1,0:T(8,128)(2,1)} %queries_ref.1, bf16[128,512]{1,0:T(8,128)(2,1)} %keys_ref.1, bf16[128,512]{1,0:T(8,128)(2,1)} %values_ref.1), custom_call_target="tpu_custom_call" | custom-call | tf_op jit(solution)/shard_map/pallas_call | solution.py:374
  2.4 0.0 copy-start.4
  2.4 0.0 copy-start.6
  2.4 9.3 %all-to-all-start = ((bf16[8,16,1024]{2,1,0:T(8,128)(2,1)}), bf16[8,16,1024]{2,1,0:T(8,128)(2,1)S(1)}, u32[]{:S(2)}, u32[]{:S(2)}) async-start(bf16[8,16,1024]{2,1,0:T(8,128)(2,1)} %get-tuple-element.20), calls=%async_computation | async-start | bytes 524288 | tf_op jit(solution)/shard_map/all_to_all | solution.py:385
  11.7 1.9 %collective-permute-start = (bf16[128,384]{1,0:T(8,128)(2,1)}, bf16[128,384]{1,0:T(8,128)(2,1)S(1)}, u32[]{:S(2)}, u32[]{:S(2)}) collective-permute-start(bf16[128,384]{1,0:T(8,128)(2,1)} %get-tuple-element.15), channel_id=1, source_target_pairs={{0,4},{4,0},{8,12},{12,8},{16,20},{20,16},{24,28},{28,24},{32,36},... | collective-permute-start | bytes 294920 | tf_op jit(solution)/shard_map/ppermute | solution.py:387
  13.6 2.7 %collective-permute-start.1 = (bf16[128,384]{1,0:T(8,128)(2,1)}, bf16[128,384]{1,0:T(8,128)(2,1)S(1)}, u32[]{:S(2)}, u32[]{:S(2)}) collective-permute-start(bf16[128,384]{1,0:T(8,128)(2,1)} %get-tuple-element.16), channel_id=1, source_target_pairs={{0,8},{4,12},{8,0},{12,4},{16,24},{20,28},{24,16},{28,20},{32,40},... | collective-permute-start | bytes 294920 | tf_op jit(solution)/shard_map/ppermute | solution.py:387
  16.3 3.0 %collective-permute-start.2 = (bf16[128,384]{1,0:T(8,128)(2,1)}, bf16[128,384]{1,0:T(8,128)(2,1)S(1)}, u32[]{:S(2)}, u32[]{:S(2)}) collective-permute-start(bf16[128,384]{1,0:T(8,128)(2,1)} %get-tuple-element.17), channel_id=1, source_target_pairs={{0,12},{4,8},{8,4},{12,0},{16,28},{20,24},{24,20},{28,16},{32,44},... | collective-permute-start | bytes 294920 | tf_op jit(solution)/shard_map/ppermute | solution.py:387
  19.3 0.0 collective-permute-done.one_ref.refs_0_
  19.3 1.6 %collective-permute-done.1.two_ref.refs_1_ = bf16[128,384]{1,0:T(8,128)(2,1)S(1)} collective-permute-done((bf16[128,384]{1,0:T(8,128)(2,1)}, bf16[128,384]{1,0:T(8,128)(2,1)S(1)}, u32[]{:S(2)}, u32[]{:S(2)}) %collective-permute-start.1) | collective-permute-done | bytes 98336 | tf_op jit(solution)/shard_map/ppermute | solution.py:387
  20.9 2.3 %collective-permute-done.2.three_ref.refs_2_ = bf16[128,384]{1,0:T(8,128)(2,1)S(1)} collective-permute-done((bf16[128,384]{1,0:T(8,128)(2,1)}, bf16[128,384]{1,0:T(8,128)(2,1)S(1)}, u32[]{:S(2)}, u32[]{:S(2)}) %collective-permute-start.2) | collective-permute-done | bytes 98336 | tf_op jit(solution)/shard_map/ppermute | solution.py:387
  23.2 0.0 all-to-all-done.column_ref
  23.2 0.0 copy-start.5
  23.2 0.7 copy-done.5
  23.8 1.8 %shard_map.66 = bf16[16,64,256]{2,1,0:T(8,128)(2,1)} custom-call(s32[1]{0:T(128)} %bitcast.1.row_ref, s32[32]{0:T(128)S(1)} %copy-done.5, bf16[8,16,1024]{2,1,0:T(8,128)(2,1)S(1)} %all-to-all-done.column_ref, bf16[128,384]{1,0:T(8,128)(2,1)S(1)} %collective-permute-done.one_ref.refs_0_, bf16[128,384]{1,0:T(8,128)(2,1)S(1)} %collective-permute-done.1.two_ref.refs_1_, ...), custom_call_target="tpu_custom_call" | custom-call | tf_op jit(solution)/shard_map/pallas_call | solution.py:388
  25.6 9.5 %all-to-all-start.1 = ((bf16[16,64,256]{2,1,0:T(8,128)(2,1)}), bf16[16,64,256]{2,1,0:T(8,128)(2,1)S(1)}, u32[]{:S(2)}, u32[]{:S(2)}) async-start(bf16[16,64,256]{2,1,0:T(8,128)(2,1)} %shard_map.66), calls=%async_computation.1 | async-start | bytes 1048576 | tf_op jit(solution)/shard_map/all_to_all | solution.py:395
  35.1 0.0 copy-done.4
  35.1 1.8 %shard_map.65 = (bf16[512,384]{1,0:T(8,128)(2,1)S(1)}, bf16[320,256]{1,0:T(8,128)(2,1)}, bf16[320,256]{1,0:T(8,128)(2,1)}, bf16[512,128]{1,0:T(8,128)(2,1)S(1)}) custom-call(bf16[128,384]{1,0:T(8,128)(2,1)S(1)} %copy-done.4, bf16[128,384]{1,0:T(8,128)(2,1)S(1)} %collective-permute-done.one_ref.refs_0_, ...), custom_call_target="tpu_custom_call" | custom-call | tf_op jit(solution)/shard_map/pallas_call | solution.py:396
  36.9 0.0 copy-start.1
  36.9 0.7 copy-done.1
  37.6 4.7 %collective-permute-start.3 = (bf16[320,256]{1,0:T(8,128)(2,1)}, bf16[320,256]{1,0:T(8,128)(2,1)}, u32[]{:S(2)}, u32[]{:S(2)}) collective-permute-start(bf16[320,256]{1,0:T(8,128)(2,1)} %get-tuple-element.21), channel_id=1, source_target_pairs={{0,16},{4,20},{8,24},{12,28},{16,32},{20,36},{24,40},{28,44},{32,4... | collective-permute-start | bytes 491528 | tf_op jit(solution)/shard_map/ppermute | solution.py:409
  42.4 4.1 %collective-permute-start.4 = (bf16[320,256]{1,0:T(8,128)(2,1)}, bf16[320,256]{1,0:T(8,128)(2,1)}, u32[]{:S(2)}, u32[]{:S(2)}) collective-permute-start(bf16[320,256]{1,0:T(8,128)(2,1)} %get-tuple-element.22), channel_id=1, source_target_pairs={{16,0},{20,4},{24,8},{28,12},{32,16},{36,20},{40,24},{44,28},{48,3... | collective-permute-start | bytes 491528 | tf_op jit(solution)/shard_map/ppermute | solution.py:410
  46.5 0.0 copy-start.7
  46.5 0.0 copy-start.2
  46.5 1.0 %copy-done.2 = bf16[512,384]{1,0:T(8,128)(2,1)S(1)} copy-done((bf16[512,384]{1,0:T(8,128)(2,1)S(1)}, bf16[512,384]{1,0:T(8,128)(2,1)}, u32[]{:S(2)}) %copy-start.2) | copy-done | bytes 393240
  47.5 0.0 copy-start
  47.5 1.6 %shard_map.68.inner_ref = f32[3,512,128]{2,1,0:T(8,128)S(1)} custom-call(bf16[512,384]{1,0:T(8,128)(2,1)S(1)} %copy-done.2), custom_call_target="tpu_custom_call" | custom-call | tf_op jit(solution)/shard_map/pallas_call | solution.py:411
  49.2 7.2 %all-to-all-done.1.row_hbm = bf16[16,64,256]{2,1,0:T(8,128)(2,1)S(1)} async-done(((bf16[16,64,256]{2,1,0:T(8,128)(2,1)}), bf16[16,64,256]{2,1,0:T(8,128)(2,1)S(1)}, u32[]{:S(2)}, u32[]{:S(2)}) %all-to-all-start.1) | async-done | bytes 524320 | tf_op jit(solution)/shard_map/all_to_all | solution.py:395
  56.4 0.0 copy-done.6
  56.4 2.4 %shard_map.67.far_ref = f32[3,128,128]{2,1,0:T(8,128)S(1)} custom-call(s32[1]{0:T(128)} %bitcast.quad_ref, s32[32]{0:T(128)S(1)} %copy-done.6, bf16[512,128]{1,0:T(8,128)(2,1)S(1)} %get-tuple-element.19.query_ref, bf16[16,64,256]{2,1,0:T(8,128)(2,1)S(1)} %all-to-all-done.1.row_hbm), custom_call_target="tpu_custom_call" | custom-call | tf_op jit(solution)/shard_map/pallas_call | solution.py:418
  58.8 0.0 collective-permute-done.3.prev_hbm
  58.8 0.0 collective-permute-done.4.next_hbm
  58.8 0.0 copy-start.3
  58.8 1.0 %copy-done.3 = bf16[512,384]{1,0:T(8,128)(2,1)S(1)} copy-done((bf16[512,384]{1,0:T(8,128)(2,1)S(1)}, bf16[512,384]{1,0:T(8,128)(2,1)}, u32[]{:S(2)}) %copy-start.3) | copy-done | bytes 393240
  59.8 3.0 %shard_map.69 = bf16[512,128]{1,0:T(8,128)(2,1)S(1)} custom-call(s32[1]{0:T(128)} %bitcast.quad_ref, bf16[512,384]{1,0:T(8,128)(2,1)S(1)} %copy-done.3, bf16[512,128]{1,0:T(8,128)(2,1)S(1)} %get-tuple-element.19.query_ref, f32[3,128,128]{2,1,0:T(8,128)S(1)} %shard_map.67.far_ref, f32[3,512,128]{2,1,0:T(8,128)S(1)} %shard_map.68.inner_ref, ...), custom_call_target="tpu_custom_call" | custom-call | tf_op jit(solution)/shard_map/pallas_call | solution.py:434
  62.8 9.6 %all_to_all.20.attended_ref = bf16[4,128,128]{2,1,0:T(8,128)(2,1)S(1)} all-to-all(bf16[4,128,128]{2,1,0:T(8,128)(2,1)S(1)} %bitcast.4), channel_id=1, replica_groups=mesh['y'=8,'zh'=4,'zl'=2,'c'=2,'x'=4] {'zl','c'}, dimensions={0} | all-to-all | bytes 262144 | tf_op jit(solution)/shard_map/all_to_all | solution.py:447
  72.4 0.0 copy-done.7
  72.4 0.0 copy-done
  72.4 0.5 shard_map.70
  72.9 13.9 %all_to_all.21.parts_ref = bf16[4,144,512]{2,1,0:T(8,128)(2,1)S(1)} all-to-all(bf16[4,144,512]{2,1,0:T(8,128)(2,1)S(1)} %shard_map.70), channel_id=1, replica_groups=mesh['y'=8,'zh'=4,'zl'=2,'c'=2,'x'=4] {'x'}, dimensions={0} | all-to-all | bytes 1179648 | tf_op jit(solution)/shard_map/all_to_all | solution.py:455
  86.8 0.8 shard_map.71
Async XLA Ops:
  2.4 32.8 %copy-start.4 = (bf16[128,384]{1,0:T(8,128)(2,1)S(1)}, bf16[128,384]{1,0:T(8,128)(2,1)}, u32[]{:S(2)}) copy-start(bf16[128,384]{1,0:T(8,128)(2,1)} %get-tuple-element.14.own_ref) | copy-start | bytes 294916
  2.4 54.0 %copy-start.6 = (s32[32]{0:T(128)S(1)}, s32[32]{0:T(128)}, u32[]{:S(2)}) copy-start(s32[32]{0:T(128)} %constant.16.clone.needed_ref) | copy-start | bytes 388
  2.4 20.8 %all-to-all-start = ((bf16[8,16,1024]{2,1,0:T(8,128)(2,1)}), bf16[8,16,1024]{2,1,0:T(8,128)(2,1)S(1)}, u32[]{:S(2)}, u32[]{:S(2)}) async-start(bf16[8,16,1024]{2,1,0:T(8,128)(2,1)} %get-tuple-element.20), calls=%async_computation | async-start | bytes 524288 | tf_op jit(solution)/shard_map/all_to_all | solution.py:385
  11.7 7.6 %collective-permute-start = (bf16[128,384]{1,0:T(8,128)(2,1)}, bf16[128,384]{1,0:T(8,128)(2,1)S(1)}, u32[]{:S(2)}, u32[]{:S(2)}) collective-permute-start(bf16[128,384]{1,0:T(8,128)(2,1)} %get-tuple-element.15), channel_id=1, source_target_pairs={{0,4},{4,0},{8,12},{12,8},{16,20},{20,16},{24,28},{28,24},{32,36},... | collective-permute-start | bytes 294920 | tf_op jit(solution)/shard_map/ppermute | solution.py:387
  13.6 7.3 %collective-permute-start.1 = (bf16[128,384]{1,0:T(8,128)(2,1)}, bf16[128,384]{1,0:T(8,128)(2,1)S(1)}, u32[]{:S(2)}, u32[]{:S(2)}) collective-permute-start(bf16[128,384]{1,0:T(8,128)(2,1)} %get-tuple-element.16), channel_id=1, source_target_pairs={{0,8},{4,12},{8,0},{12,4},{16,24},{20,28},{24,16},{28,20},{32,40},... | collective-permute-start | bytes 294920 | tf_op jit(solution)/shard_map/ppermute | solution.py:387
  16.3 6.9 %collective-permute-start.2 = (bf16[128,384]{1,0:T(8,128)(2,1)}, bf16[128,384]{1,0:T(8,128)(2,1)S(1)}, u32[]{:S(2)}, u32[]{:S(2)}) collective-permute-start(bf16[128,384]{1,0:T(8,128)(2,1)} %get-tuple-element.17), channel_id=1, source_target_pairs={{0,12},{4,8},{8,4},{12,0},{16,28},{20,24},{24,20},{28,16},{32,44},... | collective-permute-start | bytes 294920 | tf_op jit(solution)/shard_map/ppermute | solution.py:387
  23.2 0.7 copy-start.5
  25.6 30.8 %all-to-all-start.1 = ((bf16[16,64,256]{2,1,0:T(8,128)(2,1)}), bf16[16,64,256]{2,1,0:T(8,128)(2,1)S(1)}, u32[]{:S(2)}, u32[]{:S(2)}) async-start(bf16[16,64,256]{2,1,0:T(8,128)(2,1)} %shard_map.66), calls=%async_computation.1 | async-start | bytes 1048576 | tf_op jit(solution)/shard_map/all_to_all | solution.py:395
  36.9 0.7 copy-start.1
  37.6 21.1 %collective-permute-start.3 = (bf16[320,256]{1,0:T(8,128)(2,1)}, bf16[320,256]{1,0:T(8,128)(2,1)}, u32[]{:S(2)}, u32[]{:S(2)}) collective-permute-start(bf16[320,256]{1,0:T(8,128)(2,1)} %get-tuple-element.21), channel_id=1, source_target_pairs={{0,16},{4,20},{8,24},{12,28},{16,32},{20,36},{24,40},{28,44},{32,4... | collective-permute-start | bytes 491528 | tf_op jit(solution)/shard_map/ppermute | solution.py:409
  42.4 16.4 %collective-permute-start.4 = (bf16[320,256]{1,0:T(8,128)(2,1)}, bf16[320,256]{1,0:T(8,128)(2,1)}, u32[]{:S(2)}, u32[]{:S(2)}) collective-permute-start(bf16[320,256]{1,0:T(8,128)(2,1)} %get-tuple-element.22), channel_id=1, source_target_pairs={{16,0},{20,4},{24,8},{28,12},{32,16},{36,20},{40,24},{44,28},{48,3... | collective-permute-start | bytes 491528 | tf_op jit(solution)/shard_map/ppermute | solution.py:410
  46.5 25.9 %copy-start.7 = (f32[512]{0:T(512)S(1)}, f32[512]{0:T(512)}, u32[]{:S(2)}) copy-start(f32[512]{0:T(512)} %param.9) | copy-start | bytes 6148
  46.5 1.0 %copy-start.2 = (bf16[512,384]{1,0:T(8,128)(2,1)S(1)}, bf16[512,384]{1,0:T(8,128)(2,1)}, u32[]{:S(2)}) copy-start(bf16[512,384]{1,0:T(8,128)(2,1)} %copy-done.1) | copy-start | bytes 1179652
  47.5 24.9 %copy-start = (bf16[512,2048]{1,0:T(8,128)(2,1)S(1)}, bf16[512,2048]{1,0:T(8,128)(2,1)}, u32[]{:S(2)}) copy-start(bf16[512,2048]{1,0:T(8,128)(2,1)} %weight_ref.1) | copy-start | bytes 6291460
  58.8 1.0 %copy-start.3 = (bf16[512,384]{1,0:T(8,128)(2,1)S(1)}, bf16[512,384]{1,0:T(8,128)(2,1)}, u32[]{:S(2)}) copy-start(bf16[512,384]{1,0:T(8,128)(2,1)} %copy-done.1) | copy-start | bytes 1179652

commit v2 on v1

--- a/solution.py
+++ b/solution.py
@@ -88,6 +88,17 @@
     return chosen == 1
 
 
+def needed_row(row, slot):
+    chosen = NEEDED[0][slot]
+    for index in range(1, 8):
+        chosen = jnp.where(row == index, NEEDED[index][slot], chosen)
+    return chosen
+
+
+def my_quad():
+    return lax.axis_index("y") * 4 + lax.axis_index("zh")
+
+
 def begin_copies(copies, sems):
     started = [
         pltpu.make_async_copy(source, target, sems.at[index])
@@ -101,10 +112,6 @@
 def wait_copies(started):
     for copy in started:
         copy.wait()
-
-
-def my_place():
-    return lax.axis_index("zl") * 2 + lax.axis_index("c")
 
 
 def other_place(step):
@@ -133,10 +140,10 @@
     wait_copies(started[2:])
 
 
-def column_kernel(row_ref, needed_ref, column_ref, *refs):
+def column_kernel(column_ref, *refs):
     out_ref = refs[-1]
-    row = row_ref[0]
-    chosen = [needed_ref[row * 4 + slot] for slot in range(4)]
+    row = lax.axis_index("y")
+    chosen = [needed_row(row, slot) for slot in range(4)]
     chosen.append(chosen[3] + 1)
     rest = jnp.concatenate([column_ref[source] for source in chosen], axis=0)
     fourth = restrict(rest, pair_sums(48, 80))
@@ -205,7 +212,7 @@
     return attend(query, jnp.concatenate(parts, axis=0), third_mask(query.shape[0], valid))
 
 
-def gather_levels(row, needed_ref, row_ref, third_ref, fourth_ref, fifth_ref, sixth_ref):
+def gather_levels(row, row_ref, third_ref, fourth_ref, fifth_ref, sixth_ref):
     wide, narrow = pair_sums(128, 256), pair_sums(64, 128)
     fifth_ref[...] = jnp.zeros_like(fifth_ref)
     for step in range(3):
@@ -226,11 +233,11 @@
     matrix = jnp.where(in_row == source, 1.0, 0.0).astype(jnp.bfloat16)
     ordered = jnp.dot(matrix, tail, preferred_element_type=jnp.float32).astype(jnp.bfloat16)
     for slot in range(3):
-        begin = pl.multiple_of(needed_ref[row * 4 + slot] * 64, 64)
+        begin = pl.multiple_of(needed_row(row, slot) * 64, 64)
         fifth_ref[pl.ds(begin, 64), :] = ordered[slot * 64 : (slot + 1) * 64]
     for begin in range(0, 256, 128):
         sixth_ref[begin : begin + 128] = restrict(fifth_ref[2 * begin : 2 * begin + 256], wide)
-    begin = pl.multiple_of(needed_ref[row * 4 + 3] * 32, 64)
+    begin = pl.multiple_of(needed_row(row, 3) * 32, 64)
     sixth_ref[pl.ds(begin, 64), :] = ordered[192:]
 
 
@@ -244,14 +251,14 @@
             inner_ref[index, rows] = member
 
 
-def far_kernel(quad_ref, needed_ref, query_ref, row_hbm, far_ref, row_ref, *refs):
+def far_kernel(query_ref, row_hbm, far_ref, row_ref, *refs):
     *levels, scratch, sems = refs
     started = begin_copies(((row_hbm, row_ref),), sems)
     wait_copies(started)
-    quad = quad_ref[0]
+    quad = my_quad()
     row = quad // 4
     third_ref, fourth_ref, fifth_ref, sixth_ref = levels
-    gather_levels(row, needed_ref, row_ref, third_ref, fourth_ref, fifth_ref, sixth_ref)
+    gather_levels(row, row_ref, third_ref, fourth_ref, fifth_ref, sixth_ref)
     state = far_piece(query_ref[496:512], sixth_ref, row // 2, 4)
     state = spread(state, scratch, 8, 2)
     state = merge_pieces(far_piece(query_ref[480:496], fifth_ref, row, 8), state)
@@ -265,12 +272,17 @@
 
 
 def attend_kernel(
-    quad_ref, x_ref, query_ref, far_ref, inner_ref, prev_hbm, next_hbm, out_ref, *refs
+    x_hbm, query_ref, far_ref, inner_hbm, prev_hbm, next_hbm, out_ref, *refs
 ):
-    prev_ref, next_ref, scratch, sems = refs
-    started = begin_copies(((prev_hbm, prev_ref), (next_hbm, next_ref)), sems)
-    wait_copies(started)
-    quad = quad_ref[0]
+    x_ref, inner_ref, prev_ref, next_ref, scratch, sems = refs
+    copies = [(prev_hbm, prev_ref), (next_hbm, next_ref)]
+    for part in range(4):
+        rows = pl.ds(part * 128, 128)
+        copies.append((x_hbm.at[rows], x_ref.at[rows]))
+    for index in range(3):
+        copies.append((inner_hbm.at[index], inner_ref.at[index]))
+    wait_copies(begin_copies(copies, sems))
+    quad = my_quad()
     has_prev = quad > 0
     has_next = quad < QUADS - 1
     x = x_ref[...]
@@ -354,7 +366,7 @@
 
 
 ANYWHERE = pl.BlockSpec(memory_space=pl.ANY)
-SCALARS = pl.BlockSpec(memory_space=pltpu.SMEM)
+IN_HBM = pl.BlockSpec(memory_space=pltpu.HBM)
 
 
 def vmem(count):
@@ -367,10 +379,6 @@
 
 def shards(queries, keys, values, norm_gain, out_weight):
     line = ("y", "zh", "zl", "c")
-    row = lax.axis_index("y").astype(jnp.int32)
-    quad = row * 4 + lax.axis_index("zh").astype(jnp.int32)
-    row, quad = row.reshape(1), quad.reshape(1)
-    needed = jnp.array([slot for slots in NEEDED for slot in slots], jnp.int32)
     column, *heads = pl.pallas_call(
         open_kernel,
         out_shape=[bf16(8, 16, 1024)] + [bf16(128, 3 * HEAD_DIM)] * 4,
@@ -388,10 +396,10 @@
     row_parts = pl.pallas_call(
         column_kernel,
         out_shape=bf16(16, 64, PAIR),
-        in_specs=[SCALARS] * 2 + vmem(1) + [ANYWHERE] * 3,
-        out_specs=vmem(1)[0],
-        compiler_params=PARAMS,
-    )(row, needed, column, *heads[1:])
+        in_specs=vmem(1) + [ANYWHERE] * 3,
+        out_specs=vmem(1)[0],
+        compiler_params=PARAMS,
+    )(column, *heads[1:])
     row_all = lax.all_to_all(row_parts, ("zh", "zl", "c"), 0, 0, tiled=True)
     x, to_next, to_prev, coarse_queries = pl.pallas_call(
         prepare_kernel,
@@ -418,7 +426,7 @@
     far = pl.pallas_call(
         far_kernel,
         out_shape=jax.ShapeDtypeStruct((3, 128, HEAD_DIM), jnp.float32),
-        in_specs=[SCALARS] * 2 + vmem(1) + [ANYWHERE],
+        in_specs=vmem(1) + [ANYWHERE],
         out_specs=vmem(1)[0],
         scratch_shapes=[
             pltpu.VMEM((16, 64, PAIR), jnp.bfloat16),
@@ -430,20 +438,22 @@
             pltpu.SemaphoreType.DMA((1,)),
         ],
         compiler_params=PARAMS,
-    )(quad, needed, coarse_queries, row_all)
+    )(coarse_queries, row_all)
     attended = pl.pallas_call(
         attend_kernel,
         out_shape=bf16(TOKENS, HEAD_DIM),
-        in_specs=[SCALARS] + vmem(4) + [ANYWHERE] * 2,
+        in_specs=[IN_HBM] + vmem(2) + [IN_HBM] * 3,
         out_specs=vmem(1)[0],
         scratch_shapes=[
+            pltpu.VMEM((TOKENS, 3 * HEAD_DIM), jnp.bfloat16),
+            pltpu.VMEM((3, TOKENS, HEAD_DIM), jnp.float32),
             pltpu.VMEM((320, PAIR), jnp.bfloat16),
             pltpu.VMEM((320, PAIR), jnp.bfloat16),
             pltpu.VMEM((3, TOKENS, HEAD_DIM), jnp.float32),
-            pltpu.SemaphoreType.DMA((2,)),
+            pltpu.SemaphoreType.DMA((9,)),
         ],
         compiler_params=PARAMS,
-    )(quad, x, coarse_queries, far, inner, from_prev, from_next)
+    )(x, coarse_queries, far, inner, from_prev, from_next)
     own = lax.all_to_all(attended.reshape(4, 128, HEAD_DIM), ("zl", "c"), 0, 0, tiled=True)
     products = pl.pallas_call(
         project_kernel,

time: 88.3 us -> 86.5 us (0.980)
  local copies, waits for them, and re-layouts: 3.39 us -> 1.76 us
  Pallas kernels: 14.2 us -> 13.2 us
    unnamed x16 -> x10, local copies, waits for them, and re-layouts: 3.39 us -> 1.76 us
  transfers between devices with their start and end apart: 7 -> 7, of which waited for: 3 -> 3; matrix products, arithmetic and copies ran while one was open for 0% -> 0% of each run, Pallas kernels for 7% -> 6%
where the time goes in v2:
time: 86.5 us; the launch traced here: 85.9 us
  starting transfers between devices  35.2 us (41%)
  blocking collectives  23.6 us (27%)
  Pallas kernels  13.2 us (15%)
  waiting for transfers between devices  11.9 us (14%)
  local copies, waits for them, and re-layouts  1.76 us (2%)
    all_to_all x1, blocking collectives, shards(): parts = lax.all_to_all(products, 'x', 0, 0, tiled=True)  13.9 us
    all_to_all x1, blocking collectives, shards(): lax.all_to_all(attended.reshape(4, 128, HEAD_DIM), ('zl', 'c'), 0, 0, til...  9.73 us
    all_to_all x1, starting transfers between devices, shards(): row_all = lax.all_to_all(row_parts, ('zh', 'zl', 'c'), 0, 0, tiled=True)  9.51 us
    all_to_all x1, starting transfers between devices, shards(): column = lax.all_to_all(column, 'y', 0, 0, tiled=True)  9.28 us
    all_to_all x1, waiting for transfers between devices, shards(): row_all = lax.all_to_all(row_parts, ('zh', 'zl', 'c'), 0, 0, tiled=True)  8.01 us
    ppermute x3, starting transfers between devices, shards(): heads[step] = lax.ppermute(heads[step], line, exchange_pairs(step))  7.57 us
    ppermute x1, starting transfers between devices, shards(): from_prev = lax.ppermute(to_next, line, shift_pairs(1))  4.73 us
    ppermute x1, starting transfers between devices, shards(): from_next = lax.ppermute(to_prev, line, shift_pairs(-1))  4.12 us
  transfers between devices with their start and end apart: 7, of which 3 were waited for; matrix products, arithmetic and copies ran while one was open for 0% of the time, Pallas kernels for 6%

profile of v2, /device:TPU:8, one launch (start us, length us, event | category | flops | bytes accessed | tf_op | source)
XLA Modules:
  0.0 85.9 jit_solution(11580552182659344428)
XLA Ops:
  0.0 2.4 %shard_map.55 = (bf16[8,16,1024]{2,1,0:T(8,128)(2,1)}, bf16[128,384]{1,0:T(8,128)(2,1)}, bf16[128,384]{1,0:T(8,128)(2,1)}, bf16[128,384]{1,0:T(8,128)(2,1)}, bf16[128,384]{1,0:T(8,128)(2,1)}) custom-call(bf16[128,512]{1,0:T(8,128)(2,1)} %queries_ref.1, bf16[128,512]{1,0:T(8,128)(2,1)} %keys_ref.1, bf16[128,512]{1,0:T(8,128)(2,1)} %values_ref.1), custom_call_target="tpu_custom_call" | custom-call | tf_op jit(solution)/shard_map/pallas_call | solution.py:382
  2.4 0.0 copy-start.3
  2.4 9.3 %all-to-all-start = ((bf16[8,16,1024]{2,1,0:T(8,128)(2,1)}), bf16[8,16,1024]{2,1,0:T(8,128)(2,1)S(1)}, u32[]{:S(2)}, u32[]{:S(2)}) async-start(bf16[8,16,1024]{2,1,0:T(8,128)(2,1)} %get-tuple-element.20), calls=%async_computation | async-start | bytes 524288 | tf_op jit(solution)/shard_map/all_to_all | solution.py:393
  11.7 1.9 %collective-permute-start = (bf16[128,384]{1,0:T(8,128)(2,1)}, bf16[128,384]{1,0:T(8,128)(2,1)S(1)}, u32[]{:S(2)}, u32[]{:S(2)}) collective-permute-start(bf16[128,384]{1,0:T(8,128)(2,1)} %get-tuple-element.15), channel_id=1, source_target_pairs={{0,4},{4,0},{8,12},{12,8},{16,20},{20,16},{24,28},{28,24},{32,36},... | collective-permute-start | bytes 294920 | tf_op jit(solution)/shard_map/ppermute | solution.py:395
  13.6 2.7 %collective-permute-start.1 = (bf16[128,384]{1,0:T(8,128)(2,1)}, bf16[128,384]{1,0:T(8,128)(2,1)S(1)}, u32[]{:S(2)}, u32[]{:S(2)}) collective-permute-start(bf16[128,384]{1,0:T(8,128)(2,1)} %get-tuple-element.16), channel_id=1, source_target_pairs={{0,8},{4,12},{8,0},{12,4},{16,24},{20,28},{24,16},{28,20},{32,40},... | collective-permute-start | bytes 294920 | tf_op jit(solution)/shard_map/ppermute | solution.py:395
  16.3 3.0 %collective-permute-start.2 = (bf16[128,384]{1,0:T(8,128)(2,1)}, bf16[128,384]{1,0:T(8,128)(2,1)S(1)}, u32[]{:S(2)}, u32[]{:S(2)}) collective-permute-start(bf16[128,384]{1,0:T(8,128)(2,1)} %get-tuple-element.17), channel_id=1, source_target_pairs={{0,12},{4,8},{8,4},{12,0},{16,28},{20,24},{24,20},{28,16},{32,44},... | collective-permute-start | bytes 294920 | tf_op jit(solution)/shard_map/ppermute | solution.py:395
  19.3 0.0 collective-permute-done.one_ref.refs_0_
  19.3 1.6 %collective-permute-done.1.two_ref.refs_1_ = bf16[128,384]{1,0:T(8,128)(2,1)S(1)} collective-permute-done((bf16[128,384]{1,0:T(8,128)(2,1)}, bf16[128,384]{1,0:T(8,128)(2,1)S(1)}, u32[]{:S(2)}, u32[]{:S(2)}) %collective-permute-start.1) | collective-permute-done | bytes 98336 | tf_op jit(solution)/shard_map/ppermute | solution.py:395
  20.9 2.3 %collective-permute-done.2.three_ref.refs_2_ = bf16[128,384]{1,0:T(8,128)(2,1)S(1)} collective-permute-done((bf16[128,384]{1,0:T(8,128)(2,1)}, bf16[128,384]{1,0:T(8,128)(2,1)S(1)}, u32[]{:S(2)}, u32[]{:S(2)}) %collective-permute-start.2) | collective-permute-done | bytes 98336 | tf_op jit(solution)/shard_map/ppermute | solution.py:395
  23.2 0.0 all-to-all-done.column_ref
  23.2 1.2 %shard_map.57 = bf16[16,64,256]{2,1,0:T(8,128)(2,1)} custom-call(bf16[8,16,1024]{2,1,0:T(8,128)(2,1)S(1)} %all-to-all-done.column_ref, bf16[128,384]{1,0:T(8,128)(2,1)S(1)} %collective-permute-done.one_ref.refs_0_, bf16[128,384]{1,0:T(8,128)(2,1)S(1)} %collective-permute-done.1.two_ref.refs_1_, bf16[128,384]{1,0:T(8,128)(2,1)S(1)} %collective-permute-done.2.three_ref.refs_2_), custom_call_target="tpu_custom_call" | custom-call | tf_op jit(solution)/shard_map/pallas_call | solution.py:396
  24.4 9.5 %all-to-all-start.1 = ((bf16[16,64,256]{2,1,0:T(8,128)(2,1)}), bf16[16,64,256]{2,1,0:T(8,128)(2,1)S(1)}, u32[]{:S(2)}, u32[]{:S(2)}) async-start(bf16[16,64,256]{2,1,0:T(8,128)(2,1)} %shard_map.57), calls=%async_computation.1 | async-start | bytes 1048576 | tf_op jit(solution)/shard_map/all_to_all | solution.py:403
  33.9 0.0 copy-done.3
  33.9 1.7 %shard_map.56 = (bf16[512,384]{1,0:T(8,128)(2,1)S(1)}, bf16[320,256]{1,0:T(8,128)(2,1)}, bf16[320,256]{1,0:T(8,128)(2,1)}, bf16[512,128]{1,0:T(8,128)(2,1)S(1)}) custom-call(bf16[128,384]{1,0:T(8,128)(2,1)S(1)} %copy-done.3, bf16[128,384]{1,0:T(8,128)(2,1)S(1)} %collective-permute-done.one_ref.refs_0_, ...), custom_call_target="tpu_custom_call" | custom-call | tf_op jit(solution)/shard_map/pallas_call | solution.py:404
  35.7 4.7 %collective-permute-start.3 = (bf16[320,256]{1,0:T(8,128)(2,1)}, bf16[320,256]{1,0:T(8,128)(2,1)}, u32[]{:S(2)}, u32[]{:S(2)}) collective-permute-start(bf16[320,256]{1,0:T(8,128)(2,1)} %get-tuple-element.21), channel_id=1, source_target_pairs={{0,16},{4,20},{8,24},{12,28},{16,32},{20,36},{24,40},{28,44},{32,4... | collective-permute-start | bytes 491528 | tf_op jit(solution)/shard_map/ppermute | solution.py:417
  40.4 0.0 copy-start.4
  40.4 4.1 %collective-permute-start.4 = (bf16[320,256]{1,0:T(8,128)(2,1)}, bf16[320,256]{1,0:T(8,128)(2,1)}, u32[]{:S(2)}, u32[]{:S(2)}) collective-permute-start(bf16[320,256]{1,0:T(8,128)(2,1)} %get-tuple-element.22), channel_id=1, source_target_pairs={{16,0},{20,4},{24,8},{28,12},{32,16},{36,20},{40,24},{44,28},{48,3... | collective-permute-start | bytes 491528 | tf_op jit(solution)/shard_map/ppermute | solution.py:418
  44.6 0.0 copy-start
  44.6 1.6 %shard_map.59.inner_hbm = f32[3,512,128]{2,1,0:T(8,128)S(1)} custom-call(bf16[512,384]{1,0:T(8,128)(2,1)S(1)} %get-tuple-element.18.x_ref.x_hbm), custom_call_target="tpu_custom_call" | custom-call | tf_op jit(solution)/shard_map/pallas_call | solution.py:419
  46.2 0.0 copy-start.1
  46.2 0.7 copy-done.1
  47.0 8.0 %all-to-all-done.1.row_hbm = bf16[16,64,256]{2,1,0:T(8,128)(2,1)S(1)} async-done(((bf16[16,64,256]{2,1,0:T(8,128)(2,1)}), bf16[16,64,256]{2,1,0:T(8,128)(2,1)S(1)}, u32[]{:S(2)}, u32[]{:S(2)}) %all-to-all-start.1) | async-done | bytes 524320 | tf_op jit(solution)/shard_map/all_to_all | solution.py:403
  55.0 1.8 %shard_map.58.far_ref = f32[3,128,128]{2,1,0:T(8,128)S(1)} custom-call(bf16[512,128]{1,0:T(8,128)(2,1)S(1)} %get-tuple-element.19.query_ref, bf16[16,64,256]{2,1,0:T(8,128)(2,1)S(1)} %all-to-all-done.1.row_hbm), custom_call_target="tpu_custom_call" | custom-call | tf_op jit(solution)/shard_map/pallas_call | solution.py:426
  56.8 0.0 collective-permute-done.3.prev_hbm
  56.8 0.0 collective-permute-done.4.next_hbm
  56.8 0.0 copy-start.2
  56.9 1.0 %copy-done.2 = bf16[512,384]{1,0:T(8,128)(2,1)S(1)} copy-done((bf16[512,384]{1,0:T(8,128)(2,1)S(1)}, bf16[512,384]{1,0:T(8,128)(2,1)}, u32[]{:S(2)}) %copy-start.2) | copy-done | bytes 393240
  57.8 3.1 %shard_map.60 = bf16[512,128]{1,0:T(8,128)(2,1)S(1)} custom-call(bf16[512,384]{1,0:T(8,128)(2,1)S(1)} %copy-done.2, bf16[512,128]{1,0:T(8,128)(2,1)S(1)} %get-tuple-element.19.query_ref, f32[3,128,128]{2,1,0:T(8,128)S(1)} %shard_map.58.far_ref, f32[3,512,128]{2,1,0:T(8,128)S(1)} %shard_map.59.inner_hbm, bf16[320,256]{1,0:T(8,128)(2,1)} %collective-permute-done.3.prev_hbm, ...), custom_call_target="tpu_custom_call" | custom-call | tf_op jit(solution)/shard_map/pallas_call | solution.py:442
  61.0 9.7 %all_to_all.20.attended_ref = bf16[4,128,128]{2,1,0:T(8,128)(2,1)S(1)} all-to-all(bf16[4,128,128]{2,1,0:T(8,128)(2,1)S(1)} %bitcast.2), channel_id=1, replica_groups=mesh['y'=8,'zh'=4,'zl'=2,'c'=2,'x'=4] {'zl','c'}, dimensions={0} | all-to-all | bytes 262144 | tf_op jit(solution)/shard_map/all_to_all | solution.py:457
  70.7 0.0 copy-done.4
  70.7 0.0 copy-done
  70.7 0.5 shard_map.61
  71.1 13.9 %all_to_all.21.parts_ref = bf16[4,144,512]{2,1,0:T(8,128)(2,1)S(1)} all-to-all(bf16[4,144,512]{2,1,0:T(8,128)(2,1)S(1)} %shard_map.61), channel_id=1, replica_groups=mesh['y'=8,'zh'=4,'zl'=2,'c'=2,'x'=4] {'x'}, dimensions={0} | all-to-all | bytes 1179648 | tf_op jit(solution)/shard_map/all_to_all | solution.py:465
  85.1 0.8 shard_map.62
Async XLA Ops:
  2.4 31.6 %copy-start.3 = (bf16[128,384]{1,0:T(8,128)(2,1)S(1)}, bf16[128,384]{1,0:T(8,128)(2,1)}, u32[]{:S(2)}) copy-start(bf16[128,384]{1,0:T(8,128)(2,1)} %get-tuple-element.14.own_ref) | copy-start | bytes 294916
  2.4 20.8 %all-to-all-start = ((bf16[8,16,1024]{2,1,0:T(8,128)(2,1)}), bf16[8,16,1024]{2,1,0:T(8,128)(2,1)S(1)}, u32[]{:S(2)}, u32[]{:S(2)}) async-start(bf16[8,16,1024]{2,1,0:T(8,128)(2,1)} %get-tuple-element.20), calls=%async_computation | async-start | bytes 524288 | tf_op jit(solution)/shard_map/all_to_all | solution.py:393
  11.7 7.6 %collective-permute-start = (bf16[128,384]{1,0:T(8,128)(2,1)}, bf16[128,384]{1,0:T(8,128)(2,1)S(1)}, u32[]{:S(2)}, u32[]{:S(2)}) collective-permute-start(bf16[128,384]{1,0:T(8,128)(2,1)} %get-tuple-element.15), channel_id=1, source_target_pairs={{0,4},{4,0},{8,12},{12,8},{16,20},{20,16},{24,28},{28,24},{32,36},... | collective-permute-start | bytes 294920 | tf_op jit(solution)/shard_map/ppermute | solution.py:395
  13.6 7.3 %collective-permute-start.1 = (bf16[128,384]{1,0:T(8,128)(2,1)}, bf16[128,384]{1,0:T(8,128)(2,1)S(1)}, u32[]{:S(2)}, u32[]{:S(2)}) collective-permute-start(bf16[128,384]{1,0:T(8,128)(2,1)} %get-tuple-element.16), channel_id=1, source_target_pairs={{0,8},{4,12},{8,0},{12,4},{16,24},{20,28},{24,16},{28,20},{32,40},... | collective-permute-start | bytes 294920 | tf_op jit(solution)/shard_map/ppermute | solution.py:395
  16.3 6.9 %collective-permute-start.2 = (bf16[128,384]{1,0:T(8,128)(2,1)}, bf16[128,384]{1,0:T(8,128)(2,1)S(1)}, u32[]{:S(2)}, u32[]{:S(2)}) collective-permute-start(bf16[128,384]{1,0:T(8,128)(2,1)} %get-tuple-element.17), channel_id=1, source_target_pairs={{0,12},{4,8},{8,4},{12,0},{16,28},{20,24},{24,20},{28,16},{32,44},... | collective-permute-start | bytes 294920 | tf_op jit(solution)/shard_map/ppermute | solution.py:395
  24.4 30.6 %all-to-all-start.1 = ((bf16[16,64,256]{2,1,0:T(8,128)(2,1)}), bf16[16,64,256]{2,1,0:T(8,128)(2,1)S(1)}, u32[]{:S(2)}, u32[]{:S(2)}) async-start(bf16[16,64,256]{2,1,0:T(8,128)(2,1)} %shard_map.57), calls=%async_computation.1 | async-start | bytes 1048576 | tf_op jit(solution)/shard_map/all_to_all | solution.py:403
  35.7 21.1 %collective-permute-start.3 = (bf16[320,256]{1,0:T(8,128)(2,1)}, bf16[320,256]{1,0:T(8,128)(2,1)}, u32[]{:S(2)}, u32[]{:S(2)}) collective-permute-start(bf16[320,256]{1,0:T(8,128)(2,1)} %get-tuple-element.21), channel_id=1, source_target_pairs={{0,16},{4,20},{8,24},{12,28},{16,32},{20,36},{24,40},{28,44},{32,4... | collective-permute-start | bytes 491528 | tf_op jit(solution)/shard_map/ppermute | solution.py:417
  40.4 30.2 %copy-start.4 = (f32[512]{0:T(512)S(1)}, f32[512]{0:T(512)}, u32[]{:S(2)}) copy-start(f32[512]{0:T(512)} %param.8) | copy-start | bytes 6148
  40.4 16.4 %collective-permute-start.4 = (bf16[320,256]{1,0:T(8,128)(2,1)}, bf16[320,256]{1,0:T(8,128)(2,1)}, u32[]{:S(2)}, u32[]{:S(2)}) collective-permute-start(bf16[320,256]{1,0:T(8,128)(2,1)} %get-tuple-element.22), channel_id=1, source_target_pairs={{16,0},{20,4},{24,8},{28,12},{32,16},{36,20},{40,24},{44,28},{48,3... | collective-permute-start | bytes 491528 | tf_op jit(solution)/shard_map/ppermute | solution.py:418
  44.6 26.1 %copy-start = (bf16[512,2048]{1,0:T(8,128)(2,1)S(1)}, bf16[512,2048]{1,0:T(8,128)(2,1)}, u32[]{:S(2)}) copy-start(bf16[512,2048]{1,0:T(8,128)(2,1)} %weight_ref.1) | copy-start | bytes 6291460
  46.2 0.8 copy-start.1
  56.8 1.0 %copy-start.2 = (bf16[512,384]{1,0:T(8,128)(2,1)S(1)}, bf16[512,384]{1,0:T(8,128)(2,1)}, u32[]{:S(2)}) copy-start(bf16[512,384]{1,0:T(8,128)(2,1)} %copy-done.1) | copy-start | bytes 1179652

commit v3 on v2

--- a/solution.py
+++ b/solution.py
@@ -251,7 +251,8 @@
             inner_ref[index, rows] = member
 
 
-def far_kernel(query_ref, row_hbm, far_ref, row_ref, *refs):
+def far_kernel(query_ref, row_hbm, later_hbm, far_ref, row_ref, *refs):
+    del later_hbm
     *levels, scratch, sems = refs
     started = begin_copies(((row_hbm, row_ref),), sems)
     wait_copies(started)
@@ -426,7 +427,7 @@
     far = pl.pallas_call(
         far_kernel,
         out_shape=jax.ShapeDtypeStruct((3, 128, HEAD_DIM), jnp.float32),
-        in_specs=vmem(1) + [ANYWHERE],
+        in_specs=vmem(1) + [ANYWHERE] * 2,
         out_specs=vmem(1)[0],
         scratch_shapes=[
             pltpu.VMEM((16, 64, PAIR), jnp.bfloat16),
@@ -438,7 +439,7 @@
             pltpu.SemaphoreType.DMA((1,)),
         ],
         compiler_params=PARAMS,
-    )(coarse_queries, row_all)
+    )(coarse_queries, row_all, x)
     attended = pl.pallas_call(
         attend_kernel,
         out_shape=bf16(TOKENS, HEAD_DIM),

time: 86.5 us -> 86.6 us (level)
  local copies, waits for them, and re-layouts: 1.76 us -> 0.02 us
  Pallas kernels: 13.2 us -> 14.2 us
    unnamed x10 -> x6, local copies, waits for them, and re-layouts: 1.76 us -> 0.02 us
    pallas_call x1, Pallas kernels: 1.82 us -> 2.82 us  [shards(): pl.pallas_call(far_kernel, out_shape=jax.ShapeDtypeStruct((3, 128, HEAD_D...]
  transfers between devices with their start and end apart: 7 -> 7, of which waited for: 3 -> 3; matrix products, arithmetic and copies ran while one was open for 0% -> 0% of each run, Pallas kernels for 6% -> 7%
where the time goes in v3:
time: 86.6 us; the launch traced here: 86 us
  starting transfers between devices  35.3 us (41%)
  blocking collectives  23.6 us (27%)
  Pallas kernels  14.2 us (16%)
  waiting for transfers between devices  12.7 us (15%)
    all_to_all x1, blocking collectives, shards(): parts = lax.all_to_all(products, 'x', 0, 0, tiled=True)  13.9 us
    all_to_all x1, blocking collectives, shards(): lax.all_to_all(attended.reshape(4, 128, HEAD_DIM), ('zl', 'c'), 0, 0, til...  9.68 us
    all_to_all x1, starting transfers between devices, shards(): row_all = lax.all_to_all(row_parts, ('zh', 'zl', 'c'), 0, 0, tiled=True)  9.56 us
    all_to_all x1, starting transfers between devices, shards(): column = lax.all_to_all(column, 'y', 0, 0, tiled=True)  9.28 us
    all_to_all x1, waiting for transfers between devices, shards(): row_all = lax.all_to_all(row_parts, ('zh', 'zl', 'c'), 0, 0, tiled=True)  8.84 us
    ppermute x3, starting transfers between devices, shards(): heads[step] = lax.ppermute(heads[step], line, exchange_pairs(step))  7.57 us
    ppermute x1, starting transfers between devices, shards(): from_prev = lax.ppermute(to_next, line, shift_pairs(1))  4.68 us
    ppermute x1, starting transfers between devices, shards(): from_next = lax.ppermute(to_prev, line, shift_pairs(-1))  4.17 us
  transfers between devices with their start and end apart: 7, of which 3 were waited for; matrix products, arithmetic and copies ran while one was open for 0% of the time, Pallas kernels for 7%

profile of v3, /device:TPU:8, one launch (start us, length us, event | category | flops | bytes accessed | tf_op | source)
XLA Modules:
  0.0 86.0 jit_solution(9949930787279570737)
XLA Ops:
  0.0 2.4 %shard_map.55 = (bf16[8,16,1024]{2,1,0:T(8,128)(2,1)}, bf16[128,384]{1,0:T(8,128)(2,1)}, bf16[128,384]{1,0:T(8,128)(2,1)}, bf16[128,384]{1,0:T(8,128)(2,1)}, bf16[128,384]{1,0:T(8,128)(2,1)}) custom-call(bf16[128,512]{1,0:T(8,128)(2,1)} %queries_ref.1, bf16[128,512]{1,0:T(8,128)(2,1)} %keys_ref.1, bf16[128,512]{1,0:T(8,128)(2,1)} %values_ref.1), custom_call_target="tpu_custom_call" | custom-call | tf_op jit(solution)/shard_map/pallas_call | solution.py:383
  2.4 0.0 copy-start.1
  2.4 9.3 %all-to-all-start = ((bf16[8,16,1024]{2,1,0:T(8,128)(2,1)}), bf16[8,16,1024]{2,1,0:T(8,128)(2,1)S(1)}, u32[]{:S(2)}, u32[]{:S(2)}) async-start(bf16[8,16,1024]{2,1,0:T(8,128)(2,1)} %get-tuple-element.20), calls=%async_computation | async-start | bytes 524288 | tf_op jit(solution)/shard_map/all_to_all | solution.py:394
  11.7 1.9 %collective-permute-start = (bf16[128,384]{1,0:T(8,128)(2,1)}, bf16[128,384]{1,0:T(8,128)(2,1)S(1)}, u32[]{:S(2)}, u32[]{:S(2)}) collective-permute-start(bf16[128,384]{1,0:T(8,128)(2,1)} %get-tuple-element.15), channel_id=1, source_target_pairs={{0,4},{4,0},{8,12},{12,8},{16,20},{20,16},{24,28},{28,24},{32,36},... | collective-permute-start | bytes 294920 | tf_op jit(solution)/shard_map/ppermute | solution.py:396
  13.6 2.7 %collective-permute-start.1 = (bf16[128,384]{1,0:T(8,128)(2,1)}, bf16[128,384]{1,0:T(8,128)(2,1)S(1)}, u32[]{:S(2)}, u32[]{:S(2)}) collective-permute-start(bf16[128,384]{1,0:T(8,128)(2,1)} %get-tuple-element.16), channel_id=1, source_target_pairs={{0,8},{4,12},{8,0},{12,4},{16,24},{20,28},{24,16},{28,20},{32,40},... | collective-permute-start | bytes 294920 | tf_op jit(solution)/shard_map/ppermute | solution.py:396
  16.3 3.0 %collective-permute-start.2 = (bf16[128,384]{1,0:T(8,128)(2,1)}, bf16[128,384]{1,0:T(8,128)(2,1)S(1)}, u32[]{:S(2)}, u32[]{:S(2)}) collective-permute-start(bf16[128,384]{1,0:T(8,128)(2,1)} %get-tuple-element.17), channel_id=1, source_target_pairs={{0,12},{4,8},{8,4},{12,0},{16,28},{20,24},{24,20},{28,16},{32,44},... | collective-permute-start | bytes 294920 | tf_op jit(solution)/shard_map/ppermute | solution.py:396
  19.3 0.0 collective-permute-done.one_ref.refs_0_
  19.3 1.6 %collective-permute-done.1.two_ref.refs_1_ = bf16[128,384]{1,0:T(8,128)(2,1)S(1)} collective-permute-done((bf16[128,384]{1,0:T(8,128)(2,1)}, bf16[128,384]{1,0:T(8,128)(2,1)S(1)}, u32[]{:S(2)}, u32[]{:S(2)}) %collective-permute-start.1) | collective-permute-done | bytes 98336 | tf_op jit(solution)/shard_map/ppermute | solution.py:396
  20.9 2.3 %collective-permute-done.2.three_ref.refs_2_ = bf16[128,384]{1,0:T(8,128)(2,1)S(1)} collective-permute-done((bf16[128,384]{1,0:T(8,128)(2,1)}, bf16[128,384]{1,0:T(8,128)(2,1)S(1)}, u32[]{:S(2)}, u32[]{:S(2)}) %collective-permute-start.2) | collective-permute-done | bytes 98336 | tf_op jit(solution)/shard_map/ppermute | solution.py:396
  23.2 0.0 all-to-all-done.column_ref
  23.2 1.2 %shard_map.57 = bf16[16,64,256]{2,1,0:T(8,128)(2,1)} custom-call(bf16[8,16,1024]{2,1,0:T(8,128)(2,1)S(1)} %all-to-all-done.column_ref, bf16[128,384]{1,0:T(8,128)(2,1)S(1)} %collective-permute-done.one_ref.refs_0_, bf16[128,384]{1,0:T(8,128)(2,1)S(1)} %collective-permute-done.1.two_ref.refs_1_, bf16[128,384]{1,0:T(8,128)(2,1)S(1)} %collective-permute-done.2.three_ref.refs_2_), custom_call_target="tpu_custom_call" | custom-call | tf_op jit(solution)/shard_map/pallas_call | solution.py:397
  24.4 9.6 %all-to-all-start.1 = ((bf16[16,64,256]{2,1,0:T(8,128)(2,1)}), bf16[16,64,256]{2,1,0:T(8,128)(2,1)}, u32[]{:S(2)}, u32[]{:S(2)}) async-start(bf16[16,64,256]{2,1,0:T(8,128)(2,1)} %shard_map.57), calls=%async_computation.1 | async-start | bytes 1048576 | tf_op jit(solution)/shard_map/all_to_all | solution.py:404
  34.0 0.0 copy-done.1
  34.0 1.8 %shard_map.56 = (bf16[512,384]{1,0:T(8,128)(2,1)S(1)}, bf16[320,256]{1,0:T(8,128)(2,1)}, bf16[320,256]{1,0:T(8,128)(2,1)}, bf16[512,128]{1,0:T(8,128)(2,1)S(1)}) custom-call(bf16[128,384]{1,0:T(8,128)(2,1)S(1)} %copy-done.1, bf16[128,384]{1,0:T(8,128)(2,1)S(1)} %collective-permute-done.one_ref.refs_0_, ...), custom_call_target="tpu_custom_call" | custom-call | tf_op jit(solution)/shard_map/pallas_call | solution.py:405
  35.8 4.7 %collective-permute-start.3 = (bf16[320,256]{1,0:T(8,128)(2,1)}, bf16[320,256]{1,0:T(8,128)(2,1)}, u32[]{:S(2)}, u32[]{:S(2)}) collective-permute-start(bf16[320,256]{1,0:T(8,128)(2,1)} %get-tuple-element.21), channel_id=1, source_target_pairs={{0,16},{4,20},{8,24},{12,28},{16,32},{20,36},{24,40},{28,44},{32,4... | collective-permute-start | bytes 491528 | tf_op jit(solution)/shard_map/ppermute | solution.py:418
  40.4 4.2 %collective-permute-start.4 = (bf16[320,256]{1,0:T(8,128)(2,1)}, bf16[320,256]{1,0:T(8,128)(2,1)}, u32[]{:S(2)}, u32[]{:S(2)}) collective-permute-start(bf16[320,256]{1,0:T(8,128)(2,1)} %get-tuple-element.22), channel_id=1, source_target_pairs={{16,0},{20,4},{24,8},{28,12},{32,16},{36,20},{40,24},{44,28},{48,3... | collective-permute-start | bytes 491528 | tf_op jit(solution)/shard_map/ppermute | solution.py:419
  44.6 0.0 copy-start
  44.6 0.0 copy-start.2
  44.7 1.6 %shard_map.59.inner_hbm = f32[3,512,128]{2,1,0:T(8,128)S(1)} custom-call(bf16[512,384]{1,0:T(8,128)(2,1)S(1)} %get-tuple-element.18.later_hbm.x_ref.x_hbm), custom_call_target="tpu_custom_call" | custom-call | tf_op jit(solution)/shard_map/pallas_call | solution.py:420
  46.3 8.8 %all-to-all-done.1.row_hbm = bf16[16,64,256]{2,1,0:T(8,128)(2,1)} async-done(((bf16[16,64,256]{2,1,0:T(8,128)(2,1)}), bf16[16,64,256]{2,1,0:T(8,128)(2,1)}, u32[]{:S(2)}, u32[]{:S(2)}) %all-to-all-start.1) | async-done | bytes 524320 | tf_op jit(solution)/shard_map/all_to_all | solution.py:404
  55.1 2.8 %shard_map.58.far_ref = f32[3,128,128]{2,1,0:T(8,128)S(1)} custom-call(bf16[512,128]{1,0:T(8,128)(2,1)S(1)} %get-tuple-element.19.query_ref, bf16[16,64,256]{2,1,0:T(8,128)(2,1)} %all-to-all-done.1.row_hbm, bf16[512,384]{1,0:T(8,128)(2,1)S(1)} %get-tuple-element.18.later_hbm.x_ref.x_hbm), custom_call_target="tpu_custom_call" | custom-call | tf_op jit(solution)/shard_map/pallas_call | solution.py:427
  58.0 0.0 collective-permute-done.3.prev_hbm
  58.0 0.0 collective-permute-done.4.next_hbm
  58.0 3.1 %shard_map.60 = bf16[512,128]{1,0:T(8,128)(2,1)S(1)} custom-call(bf16[512,384]{1,0:T(8,128)(2,1)S(1)} %get-tuple-element.18.later_hbm.x_ref.x_hbm, bf16[512,128]{1,0:T(8,128)(2,1)S(1)} %get-tuple-element.19.query_ref, f32[3,128,128]{2,1,0:T(8,128)S(1)} %shard_map.58.far_ref, f32[3,512,128]{2,1,0:T(8,128)S(1)} %shard_map.59.inner_hbm, ...), custom_call_target="tpu_custom_call" | custom-call | tf_op jit(solution)/shard_map/pallas_call | solution.py:443
  61.1 9.7 %all_to_all.20.attended_ref = bf16[4,128,128]{2,1,0:T(8,128)(2,1)S(1)} all-to-all(bf16[4,128,128]{2,1,0:T(8,128)(2,1)S(1)} %bitcast.2), channel_id=1, replica_groups=mesh['y'=8,'zh'=4,'zl'=2,'c'=2,'x'=4] {'zl','c'}, dimensions={0} | all-to-all | bytes 262144 | tf_op jit(solution)/shard_map/all_to_all | solution.py:458
  70.8 0.0 copy-done
  70.8 0.0 copy-done.2
  70.8 0.5 shard_map.61
  71.2 13.9 %all_to_all.21.parts_ref = bf16[4,144,512]{2,1,0:T(8,128)(2,1)S(1)} all-to-all(bf16[4,144,512]{2,1,0:T(8,128)(2,1)S(1)} %shard_map.61), channel_id=1, replica_groups=mesh['y'=8,'zh'=4,'zl'=2,'c'=2,'x'=4] {'x'}, dimensions={0} | all-to-all | bytes 1179648 | tf_op jit(solution)/shard_map/all_to_all | solution.py:466
  85.2 0.8 shard_map.62
Async XLA Ops:
  2.4 31.6 %copy-start.1 = (bf16[128,384]{1,0:T(8,128)(2,1)S(1)}, bf16[128,384]{1,0:T(8,128)(2,1)}, u32[]{:S(2)}) copy-start(bf16[128,384]{1,0:T(8,128)(2,1)} %get-tuple-element.14.own_ref) | copy-start | bytes 294916
  2.4 20.8 %all-to-all-start = ((bf16[8,16,1024]{2,1,0:T(8,128)(2,1)}), bf16[8,16,1024]{2,1,0:T(8,128)(2,1)S(1)}, u32[]{:S(2)}, u32[]{:S(2)}) async-start(bf16[8,16,1024]{2,1,0:T(8,128)(2,1)} %get-tuple-element.20), calls=%async_computation | async-start | bytes 524288 | tf_op jit(solution)/shard_map/all_to_all | solution.py:394
  11.7 7.6 %collective-permute-start = (bf16[128,384]{1,0:T(8,128)(2,1)}, bf16[128,384]{1,0:T(8,128)(2,1)S(1)}, u32[]{:S(2)}, u32[]{:S(2)}) collective-permute-start(bf16[128,384]{1,0:T(8,128)(2,1)} %get-tuple-element.15), channel_id=1, source_target_pairs={{0,4},{4,0},{8,12},{12,8},{16,20},{20,16},{24,28},{28,24},{32,36},... | collective-permute-start | bytes 294920 | tf_op jit(solution)/shard_map/ppermute | solution.py:396
  13.6 7.3 %collective-permute-start.1 = (bf16[128,384]{1,0:T(8,128)(2,1)}, bf16[128,384]{1,0:T(8,128)(2,1)S(1)}, u32[]{:S(2)}, u32[]{:S(2)}) collective-permute-start(bf16[128,384]{1,0:T(8,128)(2,1)} %get-tuple-element.16), channel_id=1, source_target_pairs={{0,8},{4,12},{8,0},{12,4},{16,24},{20,28},{24,16},{28,20},{32,40},... | collective-permute-start | bytes 294920 | tf_op jit(solution)/shard_map/ppermute | solution.py:396
  16.3 6.9 %collective-permute-start.2 = (bf16[128,384]{1,0:T(8,128)(2,1)}, bf16[128,384]{1,0:T(8,128)(2,1)S(1)}, u32[]{:S(2)}, u32[]{:S(2)}) collective-permute-start(bf16[128,384]{1,0:T(8,128)(2,1)} %get-tuple-element.17), channel_id=1, source_target_pairs={{0,12},{4,8},{8,4},{12,0},{16,28},{20,24},{24,20},{28,16},{32,44},... | collective-permute-start | bytes 294920 | tf_op jit(solution)/shard_map/ppermute | solution.py:396
  24.4 30.7 %all-to-all-start.1 = ((bf16[16,64,256]{2,1,0:T(8,128)(2,1)}), bf16[16,64,256]{2,1,0:T(8,128)(2,1)}, u32[]{:S(2)}, u32[]{:S(2)}) async-start(bf16[16,64,256]{2,1,0:T(8,128)(2,1)} %shard_map.57), calls=%async_computation.1 | async-start | bytes 1048576 | tf_op jit(solution)/shard_map/all_to_all | solution.py:404
  35.8 22.2 %collective-permute-start.3 = (bf16[320,256]{1,0:T(8,128)(2,1)}, bf16[320,256]{1,0:T(8,128)(2,1)}, u32[]{:S(2)}, u32[]{:S(2)}) collective-permute-start(bf16[320,256]{1,0:T(8,128)(2,1)} %get-tuple-element.21), channel_id=1, source_target_pairs={{0,16},{4,20},{8,24},{12,28},{16,32},{20,36},{24,40},{28,44},{32,4... | collective-permute-start | bytes 491528 | tf_op jit(solution)/shard_map/ppermute | solution.py:418
  40.4 17.5 %collective-permute-start.4 = (bf16[320,256]{1,0:T(8,128)(2,1)}, bf16[320,256]{1,0:T(8,128)(2,1)}, u32[]{:S(2)}, u32[]{:S(2)}) collective-permute-start(bf16[320,256]{1,0:T(8,128)(2,1)} %get-tuple-element.22), channel_id=1, source_target_pairs={{16,0},{20,4},{24,8},{28,12},{32,16},{36,20},{40,24},{44,28},{48,3... | collective-permute-start | bytes 491528 | tf_op jit(solution)/shard_map/ppermute | solution.py:419
  44.6 26.2 %copy-start = (bf16[512,2048]{1,0:T(8,128)(2,1)S(1)}, bf16[512,2048]{1,0:T(8,128)(2,1)}, u32[]{:S(2)}) copy-start(bf16[512,2048]{1,0:T(8,128)(2,1)} %weight_ref.1) | copy-start | bytes 6291460
  44.6 26.1 %copy-start.2 = (f32[512]{0:T(512)S(1)}, f32[512]{0:T(512)}, u32[]{:S(2)}) copy-start(f32[512]{0:T(512)} %param.8) | copy-start | bytes 6148
